TPU v7x, 256 devices: a whole 4x4x8 slice. The times are simulated.
256 devices in a mesh: pb: 32 (over z, y_hi, core), ka: 8 (over x, y_lo).
Axes of the slice: x: 4, y: 4 (y_hi: 2, y_lo: 2; y = y_hi * 2 + y_lo), z: 8, core: 2. Of those that a mesh axis runs over, the one named last changes fastest.
Arguments:
- queries: bfloat16 [32768, 128], P(('pb', 'ka')), may hold values from -4 to 4
- key_rows: bfloat16 [32768, 128], P(('pb', 'ka')), may hold values from -4 to 4
- value_rows: bfloat16 [32768, 128], P(('pb', 'ka')), may hold values from -6 to 6
- outputs: bfloat16 [32768, 128], P(('pb', 'ka')), may hold values from -3 to 3
- out_grad: bfloat16 [32768, 128], P(('pb', 'ka')), may hold values from -6 to 6
- log_sums: float32 [32768], P(('pb', 'ka')), may hold values from 3 to 6
- doc_lengths: int32 [16], replicated, may hold values from 1 to 24576, 32768 in all
- tile_allowed: int32 [16, 16], replicated, may hold values from 0 to 1, as said below
Outputs:
- query_grad: bfloat16 [32768, 128], P(('pb', 'ka'))
- key_grad: bfloat16 [32768, 128], P(('pb', 'ka'))
- value_grad: bfloat16 [32768, 128], P(('pb', 'ka'))
Inputs may be any that keep to these rules, and one draw needn't show every extreme that they name: tile_allowed is 1 on the diagonal and 0 above it.
All inputs are finite; a program needn't handle non-finite values.
Results may differ from a plain program's by a relative error of at most 0.02.
Values may be sent and summed in bfloat16 or wider, within the bound.
No kernel may reach another device: no remote copies, remote signals or barrier semaphores. Data moves between devices by JAX's collectives and lax.ppermute only.
A program may use at most 64 MiB of HBM per device.

v0:
```python
import math

import jax
import jax.numpy as jnp
import numpy as np
from jax import lax
from jax.experimental import pallas as pl
from jax.experimental.pallas import tpu as pltpu
from jax.sharding import Mesh, PartitionSpec as P

AXES = ("z", "yh", "c", "x", "yl")
SIZES = (8, 2, 2, 4, 2)
PLANE = ("yh", "x", "yl")
ROWS = 128
WIDTH = 128
NDOCS = 16
TILE = 2048
RUN = 1024
PACK = 272
LOG2E = math.log2(math.e)
SCALE = 128.0 ** -0.5
SLOTS_COST = pl.CostEstimate(flops=8000000000, bytes_accessed=4 << 20, transcendentals=0)
PAIR_COST = pl.CostEstimate(flops=9000000000, bytes_accessed=1 << 20, transcendentals=0)
BF = jnp.bfloat16
F32 = jnp.float32
ONE = jax.ShapeDtypeStruct((WIDTH, ROWS), BF)
TWO = jax.ShapeDtypeStruct((2, WIDTH, ROWS), BF)
KV = jax.ShapeDtypeStruct((16, 2 * ROWS, WIDTH), BF)


def pairs_along_z(k, both_ways, back):
    pairs = []
    for i in range(256):
        z, yh, c, x, yl = (int(v) for v in np.unravel_index(i, SIZES))
        t = z - k + 8 if both_ways and c == 1 else z + k
        if z < t < 8:
            j = int(np.ravel_multi_index((t, yh, c, x, yl), SIZES))
            pairs.append((j, i) if back else (i, j))
    return pairs


def call(body, out_shape, *args, smem=0, scratch=(), cost=None, out_specs=None):
    specs = [pl.BlockSpec(memory_space=pltpu.SMEM)] * smem
    specs += [pl.BlockSpec(memory_space=pltpu.VMEM)] * (len(args) - smem)
    return pl.pallas_call(
        body,
        out_shape=out_shape,
        in_specs=specs,
        **({} if out_specs is None else {"out_specs": out_specs}),
        scratch_shapes=scratch,
        cost_estimate=cost,
        compiler_params=pltpu.CompilerParams(vmem_limit_bytes=32 * 1024 * 1024),
    )(*args)


def split3(x):
    a = x.astype(BF)
    r = x - a.astype(F32)
    b = r.astype(BF)
    c = (r - b.astype(F32)).astype(BF)
    return a, b, c


def prep_kernel(
    q_hbm, g_hbm, o_hbm, lse_hbm, k_hbm, v_hbm, pack_ref, kv_hbm, o_s, lse_s, kv_s, sems
):
    loads = [
        pltpu.make_async_copy(k_hbm, kv_s.at[0:128], sems.at[0]),
        pltpu.make_async_copy(v_hbm, kv_s.at[128:256], sems.at[1]),
        pltpu.make_async_copy(g_hbm, pack_ref.at[128:256], sems.at[2]),
        pltpu.make_async_copy(o_hbm, o_s, sems.at[3]),
        pltpu.make_async_copy(lse_hbm, lse_s, sems.at[4]),
        pltpu.make_async_copy(q_hbm, pack_ref.at[0:128], sems.at[5]),
    ]
    for copy in loads:
        copy.start()
    loads[0].wait()
    loads[1].wait()
    stores = [pltpu.make_async_copy(kv_s, kv_hbm.at[n], sems.at[6 + n]) for n in range(16)]
    for copy in stores:
        copy.start()
    loads[2].wait()
    loads[3].wait()
    loads[4].wait()
    prod = pack_ref[128:256].astype(F32) * o_s[...].astype(F32)
    delta = jnp.sum(prod.T, axis=0, keepdims=True)
    lse2 = lse_s[...] * LOG2E
    parts = split3(lse2) + split3(delta)
    stats = [p.astype(F32) for p in parts] + [jnp.zeros((10, ROWS), F32)]
    pack_ref[256:272] = jnp.concatenate(stats, axis=0).astype(BF)
    loads[5].wait()
    for copy in stores:
        copy.wait()


def prep(*args):
    anywhere = pl.BlockSpec(memory_space=pl.ANY)
    return pl.pallas_call(
        prep_kernel,
        out_shape=(jax.ShapeDtypeStruct((PACK, WIDTH), BF), KV),
        in_specs=[anywhere] * 6,
        out_specs=(pl.BlockSpec(memory_space=pltpu.VMEM), anywhere),
        scratch_shapes=[
            pltpu.VMEM((ROWS, WIDTH), BF),
            pltpu.VMEM((1, ROWS), F32),
            pltpu.VMEM((2 * ROWS, WIDTH), BF),
            pltpu.SemaphoreType.DMA((22,)),
        ],
    )(*args)


def slot_of(s, z, c):
    k = jnp.where(s < 5, s, s - 4)
    near = jnp.where(s < 5, c == 0, c == 1)
    zq = jnp.where(near | (k == 0) | (k == 4), z + k, z - k + 8)
    return zq, jnp.where(s < 5, c, 1 - c)


def slots_kernel(
    where_ref, len_ref, allow_ref, own_ref, own_x_ref, m1_ref, m2_ref, m3_ref, m4_ref, x1_ref, x2_ref, x3_ref, x4_ref,
    q_ref, g_ref, st_ref, at_ref, live_ref,
):
    z, yh, c, off = (where_ref[i] for i in range(4))
    ends = []
    total = jnp.int32(0)
    for d in range(NDOCS):
        total = total + len_ref[d]
        ends.append(total)
    slots = (
        ((own_ref, None), (own_x_ref, None)),
        ((m1_ref, 0), (m1_ref, 1)),
        ((m2_ref, 0), (m2_ref, 1)),
        ((m3_ref, 0), (m3_ref, 1)),
        ((m4_ref, None), (x4_ref, None)),
        ((x1_ref, 0), (x1_ref, 1)),
        ((x2_ref, 0), (x2_ref, 1)),
        ((x3_ref, 0), (x3_ref, 1)),
    )
    lane = lax.broadcasted_iota(jnp.int32, (1, 2 * ROWS), 1)
    pos_all = []
    for s, halves in enumerate(slots):
        stats = []
        for half, (ref, i) in enumerate(halves):
            rows = slice(half * ROWS, (half + 1) * ROWS)
            q_ref[s, rows] = ref[0:128] if i is None else ref[i, 0:128]
            g_ref[s, rows] = ref[128:256] if i is None else ref[i, 128:256]
            stats.append((ref[256:272] if i is None else ref[i, 256:272]).astype(F32))
        st = jnp.concatenate(stats, axis=1)
        st_ref[s, 0:1] = st[0:1] + st[1:2] + st[2:3]
        st_ref[s, 1:2] = st[3:4] + st[4:5] + st[5:6]
        zq, cq = slot_of(jnp.int32(s), z, c)
        base = zq * (2 * TILE) + yh * TILE + off
        pos_all.append(
            jnp.where(lane < ROWS, base + cq * RUN + lane, base + (1 - cq) * RUN - ROWS + lane)
        )
    pos = jnp.concatenate(pos_all, axis=0)
    start = jnp.zeros_like(pos)
    for e in ends:
        start = jnp.where(pos >= e, e, start)
    for s in range(8):
        at_ref[s, 0:1] = start[s : s + 1]
        at_ref[s, 1:2] = pos[s : s + 1]
        zq, _ = slot_of(jnp.int32(s), z, c)
        low = zq * (2 * TILE) + yh * TILE + off
        low_start = jnp.int32(0)
        for e in ends:
            low_start = jnp.where(e <= low, e, low_start)
        for t in range(2):
            b = z * (2 * TILE) + t * TILE + c * RUN
            ok = allow_ref[jnp.minimum(2 * zq + yh, 15), 2 * z + t] == 1
            ok = ok & (zq < 8) & (b <= low + RUN + ROWS - 1) & (b + RUN - 1 >= low_start)
            live_ref[8 * t + s] = ok.astype(jnp.int32)
    live_ref[16] = z * (2 * TILE) + c * RUN


def slots(*args):
    block = jax.ShapeDtypeStruct((8, 2 * ROWS, WIDTH), BF)
    vmem = pl.BlockSpec(memory_space=pltpu.VMEM)
    return call(
        slots_kernel,
        (
            block,
            block,
            jax.ShapeDtypeStruct((8, 8, 2 * ROWS), F32),
            jax.ShapeDtypeStruct((8, 8, 2 * ROWS), jnp.int32),
            jax.ShapeDtypeStruct((32,), jnp.int32),
        ),
        *args,
        smem=3,
        cost=SLOTS_COST,
        out_specs=(vmem, vmem, vmem, vmem, pl.BlockSpec(memory_space=pltpu.SMEM)),
    )


def grad_kernel(
    live_ref, kv_ref, q_ref, g_ref, st_ref, at_ref,
    dkv_hbm, d0_ref, d1_ref, d2_ref, d3_ref, d4_ref, dx_ref,
    kt_s, dk_acc, dv_acc, dqt_s, out_s, sems,
):
    row = lax.broadcasted_iota(jnp.int32, (RUN, 1), 0)
    dqt_s[...] = jnp.zeros_like(dqt_s)
    stores = []
    for t in range(2):
        kt_s[...] = kv_ref[8 * t : 8 * t + 8, 0:128, :].reshape(RUN, WIDTH).T
        dk_acc[...] = jnp.zeros_like(dk_acc)
        dv_acc[...] = jnp.zeros_like(dv_acc)
        b = live_ref[16] + t * TILE

        def slot_step(s, carry):
            @pl.when(live_ref[8 * t + s] == 1)
            def _unit():
                q = q_ref[s]
                g = g_ref[s]
                lse2 = st_ref[s, 0:1]
                delta = st_ref[s, 1:2]
                start = at_ref[s, 0:1]
                pos = at_ref[s, 1:2]
                k = kv_ref[8 * t : 8 * t + 8, 0:128, :].reshape(RUN, WIDTH)
                v = kv_ref[8 * t : 8 * t + 8, 128:256, :].reshape(RUN, WIDTH)
                sc = lax.dot_general(k, q, (((1,), (1,)), ((), ())), preferred_element_type=F32)
                dp = lax.dot_general(v, g, (((1,), (1,)), ((), ())), preferred_element_type=F32)
                key = b + row
                vis = (key >= start) & (key <= pos)
                p = jnp.where(vis, jnp.exp2(sc * (SCALE * LOG2E) - lse2), 0.0)
                ds = (p * (dp - delta)).astype(BF)
                dv_acc[...] += jnp.dot(p.astype(BF), g, preferred_element_type=F32)
                dk_acc[...] += jnp.dot(ds, q, preferred_element_type=F32)
                dqt_s[s] += jnp.dot(kt_s[...], ds, preferred_element_type=F32)

            return carry

        lax.fori_loop(0, 8, slot_step, 0)
        for n in range(8):
            rows = slice(n * ROWS, (n + 1) * ROWS)
            out_s[8 * t + n, 0:128] = dk_acc[rows].astype(BF)
            out_s[8 * t + n, 128:256] = dv_acc[rows].astype(BF)
        part = pl.ds(8 * t, 8)
        stores.append(pltpu.make_async_copy(out_s.at[part], dkv_hbm.at[part], sems.at[t]))
        stores[t].start()

    def term(s, half):
        return dqt_s[s, :, half * ROWS : (half + 1) * ROWS].astype(BF)

    d0_ref[...] = term(0, 0)
    d4_ref[...] = term(4, 0)
    for k, out in enumerate((d1_ref, d2_ref, d3_ref)):
        for half in range(2):
            out[half] = term(k + 1, half)
            dx_ref[2 * k + half] = term(k + 5, half)
    dx_ref[6] = term(0, 1)
    dx_ref[7] = term(4, 1)
    for copy in stores:
        copy.wait()


def grads(*args):
    vmem = pl.BlockSpec(memory_space=pltpu.VMEM)
    return call(
        grad_kernel,
        (KV, ONE, TWO, TWO, TWO, ONE, jax.ShapeDtypeStruct((8, WIDTH, ROWS), BF)),
        *args,
        smem=1,
        out_specs=(pl.BlockSpec(memory_space=pl.ANY),) + (vmem,) * 6,
        scratch=[
            pltpu.VMEM((WIDTH, RUN), BF),
            pltpu.VMEM((RUN, WIDTH), F32),
            pltpu.VMEM((RUN, WIDTH), F32),
            pltpu.VMEM((8, WIDTH, 2 * ROWS), F32),
            pltpu.VMEM((16, 2 * ROWS, WIDTH), BF),
            pltpu.SemaphoreType.DMA((2,)),
        ],
    )


def pair_kernel(d0, d1, d2, d3, d4, got, s0, s1, s2, s3, s4):
    for k, (a, out) in enumerate(((d1, s1), (d2, s2), (d3, s3))):
        out[...] = (a[...].astype(F32) + got[2 * k : 2 * k + 2].astype(F32)).astype(BF)
    s0[...] = (d0[...].astype(F32) + got[6].astype(F32)).astype(BF)
    s4[...] = (d4[...].astype(F32) + got[7].astype(F32)).astype(BF)


def column_kernel(s0, e1, e2, e3, e4, keep, send):
    total = e1[...].astype(F32) + e2[...].astype(F32) + e3[...].astype(F32)
    keep[...] = total[0] + e4[...].astype(F32) + s0[...].astype(F32)
    send[...] = total[1].astype(BF)


def last_kernel(dkv_all, keep, got, dq_ref, dk_ref, dv_ref):
    dkv = dkv_all[0].astype(F32)
    for n in range(1, 16):
        dkv = dkv + dkv_all[n].astype(F32)
    dk_ref[...] = (dkv[:ROWS] * SCALE).astype(BF)
    dv_ref[...] = dkv[ROWS:].astype(BF)
    dq_ref[...] = ((keep[...] + got[...].astype(F32)).T * SCALE).astype(BF)


def on_device(
    queries, key_rows, value_rows, outputs, out_grad, log_sums, doc_lengths, tile_allowed
):
    z, yh, c = lax.axis_index("z"), lax.axis_index("yh"), lax.axis_index("c")
    off = (lax.axis_index("x") * 2 + lax.axis_index("yl")) * ROWS
    where = jnp.stack([z, yh, c, off]).astype(jnp.int32)

    def swap(x):
        return lax.ppermute(x, "c", [(0, 1), (1, 0)])

    def along_z(x, k, both_ways=True, back=False):
        return lax.ppermute(x, AXES, pairs_along_z(k, both_ways, back))

    own, kv_out = prep(
        queries, out_grad, outputs, log_sums.reshape(1, ROWS), key_rows, value_rows
    )
    kv = lax.all_to_all(kv_out, PLANE, 0, 0, tiled=True)
    own_x = swap(own)
    both = jnp.stack([own, own_x])
    mine = [along_z(both, k, back=True) for k in (1, 2, 3)]
    mine.append(along_z(own, 4, both_ways=False, back=True))
    theirs = [swap(m) for m in mine]

    q, g, stats, at, live = slots(
        where, doc_lengths, tile_allowed, own, own_x, *mine, *theirs
    )
    dkv, d0, d1, d2, d3, d4, dx = grads(live, kv, q, g, stats, at)
    dkv_all = lax.all_to_all(dkv, PLANE, 0, 0, tiled=True)
    s0, s1, s2, s3, s4 = call(
        pair_kernel, (ONE, TWO, TWO, TWO, ONE), d0, d1, d2, d3, d4, swap(dx), cost=PAIR_COST
    )
    e1, e2, e3 = (along_z(s, k) for k, s in ((1, s1), (2, s2), (3, s3)))
    e4 = along_z(s4, 4, both_ways=False)
    keep, send = call(
        column_kernel,
        (jax.ShapeDtypeStruct((WIDTH, ROWS), F32), ONE),
        s0, e1, e2, e3, e4,
    )
    out = jax.ShapeDtypeStruct((ROWS, WIDTH), BF)
    return call(last_kernel, (out, out, out), dkv_all, keep, swap(send))


def solution(mesh):
    fine = Mesh(mesh.devices.reshape(SIZES), AXES)
    rows, vec = P(AXES, None), P(AXES)
    return jax.shard_map(
        on_device,
        mesh=fine,
        in_specs=(rows, rows, rows, rows, rows, vec, P(), P()),
        out_specs=(rows, rows, rows),
        check_vma=False,
    )
```

profile of v0, /device:TPU:32, one launch (start us, length us, event | category | flops | bytes accessed | tf_op | source)
XLA Modules:
  0.0 68.8 jit_solution(10738037035047799406)
XLA Ops:
  0.6 2.6 %shard_map.103 = (bf16[272,128]{1,0:T(8,128)(2,1)}, bf16[16,256,128]{2,1,0:T(8,128)(2,1)}) custom-call(bf16[128,128]{1,0:T(8,128)(2,1)} %q_hbm.1, bf16[128,128]{1,0:T(8,128)(2,1)} %g_hbm.1, bf16[128,128]{1,0:T(8,128)(2,1)} %o_hbm.1, f32[1,128]{1,0:T(1,128)} %bitcast.9, bf16[128,128]{1,0:T(8,128)(2,1)} %k_hbm.1, bf16[128,128]{1,0:T(8,128)(2,1)} %v_hbm.1), custom_call_target="tpu_custom_call" | custom-call | tf_op jit(solution)/shard_map/pallas_call | solution.py:98
  3.3 0.1 collective-permute-start
  3.4 1.5 %collective-permute-done.own_x_ref = bf16[272,128]{1,0:T(8,128)(2,1)S(1)} collective-permute-done((bf16[272,128]{1,0:T(8,128)(2,1)}, bf16[272,128]{1,0:T(8,128)(2,1)S(1)}, u32[]{:S(2)}, u32[]{:S(2)}) %collective-permute-start) | collective-permute-done | bytes 69664 | tf_op jit(solution)/shard_map/ppermute | solution.py:305
  4.8 0.9 %pad_maximum_fusion = bf16[2,272,128]{2,1,0:T(8,128)(2,1)S(1)} fusion(bf16[1,272,128]{2,1,0:T(8,128)(2,1)S(1)} %bitcast.8, bf16[1,272,128]{2,1,0:T(8,128)(2,1)} %bitcast.7), kind=kLoop, calls=%fused_computation | loop fusion | flops 69632 | bytes 278528 | tf_op jit(solution)/shard_map/stack | solution.py:315
  5.7 1.3 %collective-permute-start.3 = (bf16[2,272,128]{2,1,0:T(8,128)(2,1)S(1)}, bf16[2,272,128]{2,1,0:T(8,128)(2,1)S(1)}, u32[]{:S(2)}, u32[]{:S(2)}) collective-permute-start(bf16[2,272,128]{2,1,0:T(8,128)(2,1)S(1)} %pad_maximum_fusion), channel_id=1, source_target_pairs={{96,0},{97,1},{98,2},{99,3},{100,4},{101,5},{102,6},{103,7},{168,8... | collective-permute-start | bytes 417800 | tf_op jit(solution)/shard_map/ppermute | solution.py:308
  7.0 1.3 %collective-permute-start.2 = (bf16[2,272,128]{2,1,0:T(8,128)(2,1)S(1)}, bf16[2,272,128]{2,1,0:T(8,128)(2,1)S(1)}, u32[]{:S(2)}, u32[]{:S(2)}) collective-permute-start(bf16[2,272,128]{2,1,0:T(8,128)(2,1)S(1)} %pad_maximum_fusion), channel_id=1, source_target_pairs={{64,0},{65,1},{66,2},{67,3},{68,4},{69,5},{70,6},{71,7},{200,8},{2... | collective-permute-start | bytes 417800 | tf_op jit(solution)/shard_map/ppermute | solution.py:308
  8.3 3.8 %collective-permute-start.1 = (bf16[2,272,128]{2,1,0:T(8,128)(2,1)S(1)}, bf16[2,272,128]{2,1,0:T(8,128)(2,1)S(1)}, u32[]{:S(2)}, u32[]{:S(2)}) collective-permute-start(bf16[2,272,128]{2,1,0:T(8,128)(2,1)S(1)} %pad_maximum_fusion), channel_id=1, source_target_pairs={{32,0},{33,1},{34,2},{35,3},{36,4},{37,5},{38,6},{39,7},{232,8},{2... | collective-permute-start | bytes 417800 | tf_op jit(solution)/shard_map/ppermute | solution.py:308
  12.1 0.0 copy-start
  12.1 5.4 %all-to-all-start = ((bf16[16,256,128]{2,1,0:T(8,128)(2,1)}), bf16[16,256,128]{2,1,0:T(8,128)(2,1)S(1)}, u32[]{:S(2)}, u32[]{:S(2)}) async-start(bf16[16,256,128]{2,1,0:T(8,128)(2,1)} %get-tuple-element.26), calls=%async_computation | async-start | bytes 2097152 | tf_op jit(solution)/shard_map/all_to_all | solution.py:313
  17.5 0.0 copy-done
  17.5 1.3 %collective-permute-start.4 = (bf16[272,128]{1,0:T(8,128)(2,1)S(1)}, bf16[272,128]{1,0:T(8,128)(2,1)S(1)}, u32[]{:S(2)}, u32[]{:S(2)}) collective-permute-start(bf16[272,128]{1,0:T(8,128)(2,1)S(1)} %copy-done), channel_id=1, source_target_pairs={{128,0},{129,1},{130,2},{131,3},{132,4},{133,5},{134,6},{135,7},{1... | collective-permute-start | bytes 208904 | tf_op jit(solution)/shard_map/ppermute | solution.py:308
  18.8 0.6 collective-permute-done.3.m3_ref
  19.5 0.0 collective-permute-start.7
  19.5 0.8 %collective-permute-done.2.m2_ref = bf16[2,272,128]{2,1,0:T(8,128)(2,1)S(1)} collective-permute-done((bf16[2,272,128]{2,1,0:T(8,128)(2,1)S(1)}, bf16[2,272,128]{2,1,0:T(8,128)(2,1)S(1)}, u32[]{:S(2)}, u32[]{:S(2)}) %collective-permute-start.2) | collective-permute-done | bytes 139296 | tf_op jit(solution)/shard_map/ppermute | solution.py:308
  20.3 0.8 %collective-permute-start.6 = (bf16[2,272,128]{2,1,0:T(8,128)(2,1)S(1)}, bf16[2,272,128]{2,1,0:T(8,128)(2,1)S(1)}, u32[]{:S(2)}, u32[]{:S(2)}) collective-permute-start(bf16[2,272,128]{2,1,0:T(8,128)(2,1)S(1)} %collective-permute-done.2.m2_ref), channel_id=1, source_target_pairs={{0,8},{8,0},{1,9},{9,1},{2,10},{10,2},{3,11},{11,3},{4,12},{12,4},... | collective-permute-start | bytes 417800 | tf_op jit(solution)/shard_map/ppermute | solution.py:305
  21.1 0.0 collective-permute-done.1.m1_ref
  21.1 0.0 collective-permute-start.5
  21.1 0.0 copy-start.1
  21.1 8.4 %collective-permute-done.4.m4_ref = bf16[272,128]{1,0:T(8,128)(2,1)S(1)} collective-permute-done((bf16[272,128]{1,0:T(8,128)(2,1)S(1)}, bf16[272,128]{1,0:T(8,128)(2,1)S(1)}, u32[]{:S(2)}, u32[]{:S(2)}) %collective-permute-start.4) | collective-permute-done | bytes 69664 | tf_op jit(solution)/shard_map/ppermute | solution.py:308
  29.6 0.0 collective-permute-start.8
  29.6 0.0 copy-start.2
  29.6 0.1 pad_add_fusion.where_ref
  29.6 1.2 %collective-permute-done.8.x4_ref = bf16[272,128]{1,0:T(8,128)(2,1)S(1)} collective-permute-done((bf16[272,128]{1,0:T(8,128)(2,1)S(1)}, bf16[272,128]{1,0:T(8,128)(2,1)S(1)}, u32[]{:S(2)}, u32[]{:S(2)}) %collective-permute-start.8) | collective-permute-done | bytes 69664 | tf_op jit(solution)/shard_map/ppermute | solution.py:305
  30.8 0.0 collective-permute-done.7.x3_ref
  30.8 0.0 collective-permute-done.6.x2_ref
  30.8 0.0 collective-permute-done.5.x1_ref
  30.8 0.0 copy-done.1
  30.8 0.0 copy-done.2
  30.8 1.5 %shard_map.104 = (bf16[8,256,128]{2,1,0:T(8,128)(2,1)S(1)}, bf16[8,256,128]{2,1,0:T(8,128)(2,1)S(1)}, f32[8,8,256]{2,1,0:T(8,128)S(1)}, s32[8,8,256]{2,1,0:T(8,128)S(1)}, s32[32]{0:T(128)S(1)}) custom-call(s32[4]{0:T(128)S(1)} %pad_add_fusion.where_ref, s32[16]{0:T(128)S(1)} %copy-done.2, s32[16,16]{1,0:T(8,128)S(1)} %copy-done.1, ...), custom_call_target="tpu_custom_call" | custom-call | flops 8000000000 | bytes 4194304 | tf_op jit(solution)/shard_map/pallas_call | solution.py:45
  32.4 1.8 %all-to-all-done.kv_ref = bf16[16,256,128]{2,1,0:T(8,128)(2,1)S(1)} async-done(((bf16[16,256,128]{2,1,0:T(8,128)(2,1)}), bf16[16,256,128]{2,1,0:T(8,128)(2,1)S(1)}, u32[]{:S(2)}, u32[]{:S(2)}) %all-to-all-start) | async-done | bytes 1048608 | tf_op jit(solution)/shard_map/all_to_all | solution.py:313
  34.2 6.1 %shard_map.105 = (bf16[16,256,128]{2,1,0:T(8,128)(2,1)}, bf16[128,128]{1,0:T(8,128)(2,1)S(1)}, bf16[2,128,128]{2,1,0:T(8,128)(2,1)S(1)}, bf16[2,128,128]{2,1,0:T...) custom-call(s32[32]{0:T(128)S(1)} %get-tuple-element.25.live_ref, ...), custom_call_target="tpu_custom_call" | custom-call | tf_op jit(solution)/shard_map/pallas_call | solution.py:45
  40.3 0.1 collective-permute-start.9
  40.4 8.8 %all-to-all-start.1 = ((bf16[16,256,128]{2,1,0:T(8,128)(2,1)}), bf16[16,256,128]{2,1,0:T(8,128)(2,1)S(1)}, u32[]{:S(2)}, u32[]{:S(2)}) async-start(bf16[16,256,128]{2,1,0:T(8,128)(2,1)} %get-tuple-element.31), calls=%async_computation.1 | async-start | bytes 2097152 | tf_op jit(solution)/shard_map/all_to_all | solution.py:324
  49.2 0.0 collective-permute-done.9.got
  49.2 0.1 shard_map.106
  49.3 1.9 %collective-permute-start.10 = (bf16[2,128,128]{2,1,0:T(8,128)(2,1)S(1)}, bf16[2,128,128]{2,1,0:T(8,128)(2,1)S(1)}, u32[]{:S(2)}, u32[]{:S(2)}) collective-permute-start(bf16[2,128,128]{2,1,0:T(8,128)(2,1)S(1)} %get-tuple-element.39), channel_id=1, source_target_pairs={{0,32},{1,33},{2,34},{3,35},{4,36},{5,37},{6,38},{7,39},{8,232},{9... | collective-permute-start | bytes 196616 | tf_op jit(solution)/shard_map/ppermute | solution.py:308
  51.3 1.3 %collective-permute-start.11 = (bf16[2,128,128]{2,1,0:T(8,128)(2,1)S(1)}, bf16[2,128,128]{2,1,0:T(8,128)(2,1)S(1)}, u32[]{:S(2)}, u32[]{:S(2)}) collective-permute-start(bf16[2,128,128]{2,1,0:T(8,128)(2,1)S(1)} %get-tuple-element.40), channel_id=1, source_target_pairs={{0,64},{1,65},{2,66},{3,67},{4,68},{5,69},{6,70},{7,71},{8,200},{9... | collective-permute-start | bytes 196616 | tf_op jit(solution)/shard_map/ppermute | solution.py:308
  52.6 3.5 %collective-permute-start.12 = (bf16[2,128,128]{2,1,0:T(8,128)(2,1)S(1)}, bf16[2,128,128]{2,1,0:T(8,128)(2,1)S(1)}, u32[]{:S(2)}, u32[]{:S(2)}) collective-permute-start(bf16[2,128,128]{2,1,0:T(8,128)(2,1)S(1)} %get-tuple-element.41), channel_id=1, source_target_pairs={{0,96},{1,97},{2,98},{3,99},{4,100},{5,101},{6,102},{7,103},{8,168... | collective-permute-start | bytes 196616 | tf_op jit(solution)/shard_map/ppermute | solution.py:308
  56.1 1.3 %collective-permute-start.13 = (bf16[128,128]{1,0:T(8,128)(2,1)S(1)}, bf16[128,128]{1,0:T(8,128)(2,1)S(1)}, u32[]{:S(2)}, u32[]{:S(2)}) collective-permute-start(bf16[128,128]{1,0:T(8,128)(2,1)S(1)} %get-tuple-element.42), channel_id=1, source_target_pairs={{0,128},{1,129},{2,130},{3,131},{4,132},{5,133},{6,134},{7,135},{8... | collective-permute-start | bytes 98312 | tf_op jit(solution)/shard_map/ppermute | solution.py:308
  57.4 1.6 %collective-permute-done.13.e4 = bf16[128,128]{1,0:T(8,128)(2,1)S(1)} collective-permute-done((bf16[128,128]{1,0:T(8,128)(2,1)S(1)}, bf16[128,128]{1,0:T(8,128)(2,1)S(1)}, u32[]{:S(2)}, u32[]{:S(2)}) %collective-permute-start.13) | collective-permute-done | bytes 32800 | tf_op jit(solution)/shard_map/ppermute | solution.py:308
  58.9 0.0 collective-permute-done.10.e1
  58.9 0.0 collective-permute-done.11.e2
  58.9 0.0 collective-permute-done.12.e3
  59.0 0.1 collective-permute-start.14
  59.1 1.2 %collective-permute-done.14.got = bf16[128,128]{1,0:T(8,128)(2,1)S(1)} collective-permute-done((bf16[128,128]{1,0:T(8,128)(2,1)S(1)}, bf16[128,128]{1,0:T(8,128)(2,1)S(1)}, u32[]{:S(2)}, u32[]{:S(2)}) %collective-permute-start.14) | collective-permute-done | bytes 32800 | tf_op jit(solution)/shard_map/ppermute | solution.py:305
  60.3 7.8 %all-to-all-done.1.dkv_all = bf16[16,256,128]{2,1,0:T(8,128)(2,1)S(1)} async-done(((bf16[16,256,128]{2,1,0:T(8,128)(2,1)}), bf16[16,256,128]{2,1,0:T(8,128)(2,1)S(1)}, u32[]{:S(2)}, u32[]{:S(2)}) %all-to-all-start.1) | async-done | bytes 1048608 | tf_op jit(solution)/shard_map/all_to_all | solution.py:324
  68.0 0.8 %shard_map.108 = (bf16[128,128]{1,0:T(8,128)(2,1)}, bf16[128,128]{1,0:T(8,128)(2,1)}, bf16[128,128]{1,0:T(8,128)(2,1)}) custom-call(bf16[16,256,128]{2,1,0:T(8,128)(2,1)S(1)} %all-to-all-done.1.dkv_all, f32[128,128]{1,0:T(8,128)S(1)} %get-tuple-element.43.keep, bf16[128,128]{1,0:T(8,128)(2,1)S(1)} %collective-permute-done.14.got), custom_call_target="tpu_custom_call" | custom-call | tf_op jit(solution)/shard_map/pallas_call | solution.py:45
  (1 shorter events, 0.0 us)
Async XLA Ops:
  3.3 1.6 %collective-permute-start = (bf16[272,128]{1,0:T(8,128)(2,1)}, bf16[272,128]{1,0:T(8,128)(2,1)S(1)}, u32[]{:S(2)}, u32[]{:S(2)}) collective-permute-start(bf16[272,128]{1,0:T(8,128)(2,1)} %get-tuple-element.24.own_ref), channel_id=1, source_target_pairs={{0,8},{8,0},{1,9},{9,1},{2,10},{10,2},{3,11},{11,3},{4,12},{12,4},... | collective-permute-start | bytes 208904 | tf_op jit(solution)/shard_map/ppermute | solution.py:305
  5.7 13.8 %collective-permute-start.3 = (bf16[2,272,128]{2,1,0:T(8,128)(2,1)S(1)}, bf16[2,272,128]{2,1,0:T(8,128)(2,1)S(1)}, u32[]{:S(2)}, u32[]{:S(2)}) collective-permute-start(bf16[2,272,128]{2,1,0:T(8,128)(2,1)S(1)} %pad_maximum_fusion), channel_id=1, source_target_pairs={{96,0},{97,1},{98,2},{99,3},{100,4},{101,5},{102,6},{103,7},{168,8... | collective-permute-start | bytes 417800 | tf_op jit(solution)/shard_map/ppermute | solution.py:308
  7.0 13.3 %collective-permute-start.2 = (bf16[2,272,128]{2,1,0:T(8,128)(2,1)S(1)}, bf16[2,272,128]{2,1,0:T(8,128)(2,1)S(1)}, u32[]{:S(2)}, u32[]{:S(2)}) collective-permute-start(bf16[2,272,128]{2,1,0:T(8,128)(2,1)S(1)} %pad_maximum_fusion), channel_id=1, source_target_pairs={{64,0},{65,1},{66,2},{67,3},{68,4},{69,5},{70,6},{71,7},{200,8},{2... | collective-permute-start | bytes 417800 | tf_op jit(solution)/shard_map/ppermute | solution.py:308
  8.3 12.8 %collective-permute-start.1 = (bf16[2,272,128]{2,1,0:T(8,128)(2,1)S(1)}, bf16[2,272,128]{2,1,0:T(8,128)(2,1)S(1)}, u32[]{:S(2)}, u32[]{:S(2)}) collective-permute-start(bf16[2,272,128]{2,1,0:T(8,128)(2,1)S(1)} %pad_maximum_fusion), channel_id=1, source_target_pairs={{32,0},{33,1},{34,2},{35,3},{36,4},{37,5},{38,6},{39,7},{232,8},{2... | collective-permute-start | bytes 417800 | tf_op jit(solution)/shard_map/ppermute | solution.py:308
  12.1 5.5 %copy-start = (bf16[272,128]{1,0:T(8,128)(2,1)S(1)}, bf16[272,128]{1,0:T(8,128)(2,1)}, u32[]{:S(2)}) copy-start(bf16[272,128]{1,0:T(8,128)(2,1)} %get-tuple-element.24.own_ref) | copy-start | bytes 208900
  12.1 22.1 %all-to-all-start = ((bf16[16,256,128]{2,1,0:T(8,128)(2,1)}), bf16[16,256,128]{2,1,0:T(8,128)(2,1)S(1)}, u32[]{:S(2)}, u32[]{:S(2)}) async-start(bf16[16,256,128]{2,1,0:T(8,128)(2,1)} %get-tuple-element.26), calls=%async_computation | async-start | bytes 2097152 | tf_op jit(solution)/shard_map/all_to_all | solution.py:313
  17.5 12.0 %collective-permute-start.4 = (bf16[272,128]{1,0:T(8,128)(2,1)S(1)}, bf16[272,128]{1,0:T(8,128)(2,1)S(1)}, u32[]{:S(2)}, u32[]{:S(2)}) collective-permute-start(bf16[272,128]{1,0:T(8,128)(2,1)S(1)} %copy-done), channel_id=1, source_target_pairs={{128,0},{129,1},{130,2},{131,3},{132,4},{133,5},{134,6},{135,7},{1... | collective-permute-start | bytes 208904 | tf_op jit(solution)/shard_map/ppermute | solution.py:308
  19.5 11.3 %collective-permute-start.7 = (bf16[2,272,128]{2,1,0:T(8,128)(2,1)S(1)}, bf16[2,272,128]{2,1,0:T(8,128)(2,1)S(1)}, u32[]{:S(2)}, u32[]{:S(2)}) collective-permute-start(bf16[2,272,128]{2,1,0:T(8,128)(2,1)S(1)} %collective-permute-done.3.m3_ref), channel_id=1, source_target_pairs={{0,8},{8,0},{1,9},{9,1},{2,10},{10,2},{3,11},{11,3},{4,12},{12,4},... | collective-permute-start | bytes 417800 | tf_op jit(solution)/shard_map/ppermute | solution.py:305
  20.3 10.5 %collective-permute-start.6 = (bf16[2,272,128]{2,1,0:T(8,128)(2,1)S(1)}, bf16[2,272,128]{2,1,0:T(8,128)(2,1)S(1)}, u32[]{:S(2)}, u32[]{:S(2)}) collective-permute-start(bf16[2,272,128]{2,1,0:T(8,128)(2,1)S(1)} %collective-permute-done.2.m2_ref), channel_id=1, source_target_pairs={{0,8},{8,0},{1,9},{9,1},{2,10},{10,2},{3,11},{11,3},{4,12},{12,4},... | collective-permute-start | bytes 417800 | tf_op jit(solution)/shard_map/ppermute | solution.py:305
  21.1 9.7 %collective-permute-start.5 = (bf16[2,272,128]{2,1,0:T(8,128)(2,1)S(1)}, bf16[2,272,128]{2,1,0:T(8,128)(2,1)S(1)}, u32[]{:S(2)}, u32[]{:S(2)}) collective-permute-start(bf16[2,272,128]{2,1,0:T(8,128)(2,1)S(1)} %collective-permute-done.1.m1_ref), channel_id=1, source_target_pairs={{0,8},{8,0},{1,9},{9,1},{2,10},{10,2},{3,11},{11,3},{4,12},{12,4},... | collective-permute-start | bytes 417800 | tf_op jit(solution)/shard_map/ppermute | solution.py:305
  21.1 9.7 %copy-start.1 = (s32[16,16]{1,0:T(8,128)S(1)}, s32[16,16]{1,0:T(8,128)}, u32[]{:S(2)}) copy-start(s32[16,16]{1,0:T(8,128)} %allow_ref.1) | copy-start | bytes 3076
  29.6 1.3 %collective-permute-start.8 = (bf16[272,128]{1,0:T(8,128)(2,1)S(1)}, bf16[272,128]{1,0:T(8,128)(2,1)S(1)}, u32[]{:S(2)}, u32[]{:S(2)}) collective-permute-start(bf16[272,128]{1,0:T(8,128)(2,1)S(1)} %collective-permute-done.4.m4_ref), channel_id=1, source_target_pairs={{0,8},{8,0},{1,9},{9,1},{2,10},{10,2},{3,11},{11,3},{4,12},{12,4},... | collective-permute-start | bytes 208904 | tf_op jit(solution)/shard_map/ppermute | solution.py:305
  29.6 1.3 %copy-start.2 = (s32[16]{0:T(128)S(1)}, s32[16]{0:T(128)}, u32[]{:S(2)}) copy-start(s32[16]{0:T(128)} %len_ref.1) | copy-start | bytes 196
  40.3 9.0 %collective-permute-start.9 = (bf16[8,128,128]{2,1,0:T(8,128)(2,1)S(1)}, bf16[8,128,128]{2,1,0:T(8,128)(2,1)S(1)}, u32[]{:S(2)}, u32[]{:S(2)}) collective-permute-start(bf16[8,128,128]{2,1,0:T(8,128)(2,1)S(1)} %get-tuple-element.37), channel_id=1, source_target_pairs={{0,8},{8,0},{1,9},{9,1},{2,10},{10,2},{3,11},{11,3},{4,12},{12,4},... | collective-permute-start | bytes 786440 | tf_op jit(solution)/shard_map/ppermute | solution.py:305
  40.4 27.6 %all-to-all-start.1 = ((bf16[16,256,128]{2,1,0:T(8,128)(2,1)}), bf16[16,256,128]{2,1,0:T(8,128)(2,1)S(1)}, u32[]{:S(2)}, u32[]{:S(2)}) async-start(bf16[16,256,128]{2,1,0:T(8,128)(2,1)} %get-tuple-element.31), calls=%async_computation.1 | async-start | bytes 2097152 | tf_op jit(solution)/shard_map/all_to_all | solution.py:324
  49.3 9.6 %collective-permute-start.10 = (bf16[2,128,128]{2,1,0:T(8,128)(2,1)S(1)}, bf16[2,128,128]{2,1,0:T(8,128)(2,1)S(1)}, u32[]{:S(2)}, u32[]{:S(2)}) collective-permute-start(bf16[2,128,128]{2,1,0:T(8,128)(2,1)S(1)} %get-tuple-element.39), channel_id=1, source_target_pairs={{0,32},{1,33},{2,34},{3,35},{4,36},{5,37},{6,38},{7,39},{8,232},{9... | collective-permute-start | bytes 196616 | tf_op jit(solution)/shard_map/ppermute | solution.py:308
  51.3 7.7 %collective-permute-start.11 = (bf16[2,128,128]{2,1,0:T(8,128)(2,1)S(1)}, bf16[2,128,128]{2,1,0:T(8,128)(2,1)S(1)}, u32[]{:S(2)}, u32[]{:S(2)}) collective-permute-start(bf16[2,128,128]{2,1,0:T(8,128)(2,1)S(1)} %get-tuple-element.40), channel_id=1, source_target_pairs={{0,64},{1,65},{2,66},{3,67},{4,68},{5,69},{6,70},{7,71},{8,200},{9... | collective-permute-start | bytes 196616 | tf_op jit(solution)/shard_map/ppermute | solution.py:308
  52.6 6.4 %collective-permute-start.12 = (bf16[2,128,128]{2,1,0:T(8,128)(2,1)S(1)}, bf16[2,128,128]{2,1,0:T(8,128)(2,1)S(1)}, u32[]{:S(2)}, u32[]{:S(2)}) collective-permute-start(bf16[2,128,128]{2,1,0:T(8,128)(2,1)S(1)} %get-tuple-element.41), channel_id=1, source_target_pairs={{0,96},{1,97},{2,98},{3,99},{4,100},{5,101},{6,102},{7,103},{8,168... | collective-permute-start | bytes 196616 | tf_op jit(solution)/shard_map/ppermute | solution.py:308
  56.1 2.9 %collective-permute-start.13 = (bf16[128,128]{1,0:T(8,128)(2,1)S(1)}, bf16[128,128]{1,0:T(8,128)(2,1)S(1)}, u32[]{:S(2)}, u32[]{:S(2)}) collective-permute-start(bf16[128,128]{1,0:T(8,128)(2,1)S(1)} %get-tuple-element.42), channel_id=1, source_target_pairs={{0,128},{1,129},{2,130},{3,131},{4,132},{5,133},{6,134},{7,135},{8... | collective-permute-start | bytes 98312 | tf_op jit(solution)/shard_map/ppermute | solution.py:308
  59.0 1.3 %collective-permute-start.14 = (bf16[128,128]{1,0:T(8,128)(2,1)S(1)}, bf16[128,128]{1,0:T(8,128)(2,1)S(1)}, u32[]{:S(2)}, u32[]{:S(2)}) collective-permute-start(bf16[128,128]{1,0:T(8,128)(2,1)S(1)} %get-tuple-element.44), channel_id=1, source_target_pairs={{0,8},{8,0},{1,9},{9,1},{2,10},{10,2},{3,11},{11,3},{4,12},{12,4},... | collective-permute-start | bytes 98312 | tf_op jit(solution)/shard_map/ppermute | solution.py:305
where the time goes:
time: 67.8 us; the launch traced here: 68.8 us
  starting transfers between devices  31 us (46%)
  waiting for transfers between devices  24.9 us (37%)
  Pallas kernels  11.1 us (16%)
  other arithmetic  0.97 us (1%)
  between operations  0.84 us (1%)
    ppermute x8, starting transfers between devices, along_z(): return lax.ppermute(x, AXES, pairs_along_z(k, both_ways, back))  15.6 us
    ppermute x8, waiting for transfers between devices, along_z(): return lax.ppermute(x, AXES, pairs_along_z(k, both_ways, back))  11.5 us
    all_to_all x1, starting transfers between devices, on_device(): dkv_all = lax.all_to_all(dkv, PLANE, 0, 0, tiled=True)  8.84 us
    pallas_call x5, Pallas kernels, call(): pl.pallas_call(body, out_shape=out_shape, in_specs=specs, **{} if out_spe...  8.48 us
    all_to_all x1, waiting for transfers between devices, on_device(): dkv_all = lax.all_to_all(dkv, PLANE, 0, 0, tiled=True)  7.75 us
    all_to_all x1, starting transfers between devices, on_device(): kv = lax.all_to_all(kv_out, PLANE, 0, 0, tiled=True)  5.44 us
    ppermute x7, waiting for transfers between devices, swap(): return lax.ppermute(x, 'c', [(0, 1), (1, 0)])  3.84 us
    pallas_call x1, Pallas kernels, prep(): pl.pallas_call(prep_kernel, out_shape=(jax.ShapeDtypeStruct((PACK, WIDTH)...  2.62 us
  transfers between devices with their start and end apart: 17, of which 9 were waited for; matrix products, arithmetic and copies ran while one was open for 0% of the time, Pallas kernels for 2%

commit v1 on v0

--- a/solution.py
+++ b/solution.py
@@ -19,7 +19,8 @@
 PACK = 272
 LOG2E = math.log2(math.e)
 SCALE = 128.0 ** -0.5
-SLOTS_COST = pl.CostEstimate(flops=8000000000, bytes_accessed=4 << 20, transcendentals=0)
+SLOTS_COST = pl.CostEstimate(flops=7600000000, bytes_accessed=4 << 20, transcendentals=0)
+SPREAD_COST = pl.CostEstimate(flops=10**9, bytes_accessed=2 << 20, transcendentals=0)
 PAIR_COST = pl.CostEstimate(flops=9000000000, bytes_accessed=1 << 20, transcendentals=0)
 BF = jnp.bfloat16
 F32 = jnp.float32
@@ -61,71 +62,154 @@
     return a, b, c
 
 
+def slot_of(s, z, c):
+    k = s % 5 if s < 5 else s - 4
+    if k in (0, 4):
+        return z + k, c
+    near = jnp.where(c == 0, z + k, z - k + 8)
+    far = jnp.where(c == 0, z - k + 8, z + k)
+    return (near, c) if s < 5 else (far, 1 - c)
+
+
 def prep_kernel(
-    q_hbm, g_hbm, o_hbm, lse_hbm, k_hbm, v_hbm, pack_ref, kv_hbm, o_s, lse_s, kv_s, sems
+    q_hbm, g_hbm, o_hbm, lse_hbm, len_hbm, allow_hbm,
+    pack_ref, at_ref,
+    o_s, lse_s, len_s, allow_s, sems,
 ):
     loads = [
-        pltpu.make_async_copy(k_hbm, kv_s.at[0:128], sems.at[0]),
-        pltpu.make_async_copy(v_hbm, kv_s.at[128:256], sems.at[1]),
-        pltpu.make_async_copy(g_hbm, pack_ref.at[128:256], sems.at[2]),
-        pltpu.make_async_copy(o_hbm, o_s, sems.at[3]),
-        pltpu.make_async_copy(lse_hbm, lse_s, sems.at[4]),
+        pltpu.make_async_copy(g_hbm, pack_ref.at[128:256], sems.at[0]),
+        pltpu.make_async_copy(o_hbm, o_s, sems.at[1]),
+        pltpu.make_async_copy(lse_hbm, lse_s, sems.at[2]),
+        pltpu.make_async_copy(len_hbm, len_s, sems.at[3]),
+        pltpu.make_async_copy(allow_hbm, allow_s, sems.at[4]),
         pltpu.make_async_copy(q_hbm, pack_ref.at[0:128], sems.at[5]),
     ]
     for copy in loads:
         copy.start()
-    loads[0].wait()
-    loads[1].wait()
-    stores = [pltpu.make_async_copy(kv_s, kv_hbm.at[n], sems.at[6 + n]) for n in range(16)]
-    for copy in stores:
-        copy.start()
-    loads[2].wait()
-    loads[3].wait()
-    loads[4].wait()
+    for copy in loads[:3]:
+        copy.wait()
     prod = pack_ref[128:256].astype(F32) * o_s[...].astype(F32)
     delta = jnp.sum(prod.T, axis=0, keepdims=True)
     lse2 = lse_s[...] * LOG2E
     parts = split3(lse2) + split3(delta)
     stats = [p.astype(F32) for p in parts] + [jnp.zeros((10, ROWS), F32)]
     pack_ref[256:272] = jnp.concatenate(stats, axis=0).astype(BF)
+
+    loads[3].wait()
+    loads[4].wait()
+    z, yh, c = lax.axis_index("z"), lax.axis_index("yh"), lax.axis_index("c")
+    off = (lax.axis_index("x") * 2 + lax.axis_index("yl")) * ROWS
+    ends = []
+    total = jnp.int32(0)
+    for d in range(NDOCS):
+        total = total + len_s[d]
+        ends.append(total)
+    lane = lax.broadcasted_iota(jnp.int32, (1, 2 * ROWS), 1)
+    key_base = z * (2 * TILE) + c * RUN
+    flag_lane = lax.broadcasted_iota(jnp.int32, (8, 2 * ROWS), 1)
+    live = jnp.where(flag_lane == 16, key_base, 0)
+    pos_all = []
+    for s in range(8):
+        zq, cq = slot_of(s, z, c)
+        low = zq * (2 * TILE) + yh * TILE + off
+        pos_all.append(
+            jnp.where(lane < ROWS, low + cq * RUN + lane, low + (1 - cq) * RUN - ROWS + lane)
+        )
+        low_start = jnp.int32(0)
+        for e in ends:
+            low_start = jnp.where(e <= low, e, low_start)
+        for t in range(2):
+            b = key_base + t * TILE
+            ok = allow_s[jnp.minimum(2 * zq + yh, 15), 2 * z + t] == 1
+            ok = ok & (zq < 8) & (b <= low + RUN + ROWS - 1) & (b + RUN - 1 >= low_start)
+            live = jnp.where(flag_lane == 8 * t + s, ok.astype(jnp.int32), live)
+    pos = jnp.concatenate(pos_all, axis=0)
+    start = jnp.zeros_like(pos)
+    for e in ends:
+        start = jnp.where(pos >= e, e, start)
+    for s in range(8):
+        at_ref[s, 0:1] = start[s : s + 1]
+        at_ref[s, 1:2] = pos[s : s + 1]
+    at_ref[8] = live
     loads[5].wait()
-    for copy in stores:
-        copy.wait()
 
 
 def prep(*args):
-    anywhere = pl.BlockSpec(memory_space=pl.ANY)
+    hbm = pl.BlockSpec(memory_space=pl.ANY)
+    vmem = pl.BlockSpec(memory_space=pltpu.VMEM)
     return pl.pallas_call(
         prep_kernel,
-        out_shape=(jax.ShapeDtypeStruct((PACK, WIDTH), BF), KV),
-        in_specs=[anywhere] * 6,
-        out_specs=(pl.BlockSpec(memory_space=pltpu.VMEM), anywhere),
+        out_shape=(
+            jax.ShapeDtypeStruct((PACK, WIDTH), BF),
+            jax.ShapeDtypeStruct((9, 8, 2 * ROWS), jnp.int32),
+        ),
+        in_specs=[hbm] * 6,
+        out_specs=(vmem, vmem),
         scratch_shapes=[
             pltpu.VMEM((ROWS, WIDTH), BF),
             pltpu.VMEM((1, ROWS), F32),
-            pltpu.VMEM((2 * ROWS, WIDTH), BF),
-            pltpu.SemaphoreType.DMA((22,)),
+            pltpu.SMEM((NDOCS,), jnp.int32),
+            pltpu.SMEM((16, 16), jnp.int32),
+            pltpu.SemaphoreType.DMA((6,)),
         ],
     )(*args)
 
 
-def slot_of(s, z, c):
-    k = jnp.where(s < 5, s, s - 4)
-    near = jnp.where(s < 5, c == 0, c == 1)
-    zq = jnp.where(near | (k == 0) | (k == 4), z + k, z - k + 8)
-    return zq, jnp.where(s < 5, c, 1 - c)
+def spread_kernel(k_hbm, v_hbm, kv_hbm, kv_s, sems):
+    loads = [
+        pltpu.make_async_copy(k_hbm, kv_s.at[0:128], sems.at[0]),
+        pltpu.make_async_copy(v_hbm, kv_s.at[128:256], sems.at[1]),
+    ]
+    for copy in loads:
+        copy.start()
+    for copy in loads:
+        copy.wait()
+    stores = [pltpu.make_async_copy(kv_s, kv_hbm.at[n], sems.at[2 + n]) for n in range(16)]
+    for copy in stores:
+        copy.start()
+    for copy in stores:
+        copy.wait()
+
+
+def spread(*args):
+    hbm = pl.BlockSpec(memory_space=pl.ANY)
+    return pl.pallas_call(
+        spread_kernel,
+        out_shape=KV,
+        in_specs=[hbm] * 2,
+        out_specs=hbm,
+        scratch_shapes=[pltpu.VMEM((2 * ROWS, WIDTH), BF), pltpu.SemaphoreType.DMA((18,))],
+        cost_estimate=SPREAD_COST,
+    )(*args)
+
+
+def stack_kernel(own_ref, other_ref, after, both_ref, sems):
+    copies = [
+        pltpu.make_async_copy(ref, both_ref.at[n], sems.at[n])
+        for n, ref in enumerate((own_ref, other_ref))
+    ]
+    for copy in copies:
+        copy.start()
+    for copy in copies:
+        copy.wait()
+
+
+def stack(*args):
+    hbm = pl.BlockSpec(memory_space=pl.ANY)
+    return pl.pallas_call(
+        stack_kernel,
+        out_shape=jax.ShapeDtypeStruct((2, PACK, WIDTH), BF),
+        in_specs=[hbm] * 3,
+        out_specs=pl.BlockSpec(memory_space=pltpu.VMEM),
+        scratch_shapes=[pltpu.SemaphoreType.DMA((2,))],
+        compiler_params=pltpu.CompilerParams(vmem_limit_bytes=32 * 1024 * 1024),
+    )(*args)
 
 
 def slots_kernel(
-    where_ref, len_ref, allow_ref, own_ref, own_x_ref, m1_ref, m2_ref, m3_ref, m4_ref, x1_ref, x2_ref, x3_ref, x4_ref,
-    q_ref, g_ref, st_ref, at_ref, live_ref,
+    own_ref, own_x_ref, m1_ref, m2_ref, m3_ref, m4_ref, x1_ref, x2_ref, x3_ref, x4_ref,
+    q_ref, g_ref, st_ref,
 ):
-    z, yh, c, off = (where_ref[i] for i in range(4))
-    ends = []
-    total = jnp.int32(0)
-    for d in range(NDOCS):
-        total = total + len_ref[d]
-        ends.append(total)
     slots = (
         ((own_ref, None), (own_x_ref, None)),
         ((m1_ref, 0), (m1_ref, 1)),
@@ -136,8 +220,6 @@
         ((x2_ref, 0), (x2_ref, 1)),
         ((x3_ref, 0), (x3_ref, 1)),
     )
-    lane = lax.broadcasted_iota(jnp.int32, (1, 2 * ROWS), 1)
-    pos_all = []
     for s, halves in enumerate(slots):
         stats = []
         for half, (ref, i) in enumerate(halves):
@@ -148,55 +230,21 @@
         st = jnp.concatenate(stats, axis=1)
         st_ref[s, 0:1] = st[0:1] + st[1:2] + st[2:3]
         st_ref[s, 1:2] = st[3:4] + st[4:5] + st[5:6]
-        zq, cq = slot_of(jnp.int32(s), z, c)
-        base = zq * (2 * TILE) + yh * TILE + off
-        pos_all.append(
-            jnp.where(lane < ROWS, base + cq * RUN + lane, base + (1 - cq) * RUN - ROWS + lane)
-        )
-    pos = jnp.concatenate(pos_all, axis=0)
-    start = jnp.zeros_like(pos)
-    for e in ends:
-        start = jnp.where(pos >= e, e, start)
-    for s in range(8):
-        at_ref[s, 0:1] = start[s : s + 1]
-        at_ref[s, 1:2] = pos[s : s + 1]
-        zq, _ = slot_of(jnp.int32(s), z, c)
-        low = zq * (2 * TILE) + yh * TILE + off
-        low_start = jnp.int32(0)
-        for e in ends:
-            low_start = jnp.where(e <= low, e, low_start)
-        for t in range(2):
-            b = z * (2 * TILE) + t * TILE + c * RUN
-            ok = allow_ref[jnp.minimum(2 * zq + yh, 15), 2 * z + t] == 1
-            ok = ok & (zq < 8) & (b <= low + RUN + ROWS - 1) & (b + RUN - 1 >= low_start)
-            live_ref[8 * t + s] = ok.astype(jnp.int32)
-    live_ref[16] = z * (2 * TILE) + c * RUN
 
 
 def slots(*args):
     block = jax.ShapeDtypeStruct((8, 2 * ROWS, WIDTH), BF)
-    vmem = pl.BlockSpec(memory_space=pltpu.VMEM)
-    return call(
-        slots_kernel,
-        (
-            block,
-            block,
-            jax.ShapeDtypeStruct((8, 8, 2 * ROWS), F32),
-            jax.ShapeDtypeStruct((8, 8, 2 * ROWS), jnp.int32),
-            jax.ShapeDtypeStruct((32,), jnp.int32),
-        ),
-        *args,
-        smem=3,
-        cost=SLOTS_COST,
-        out_specs=(vmem, vmem, vmem, vmem, pl.BlockSpec(memory_space=pltpu.SMEM)),
-    )
+    stats = jax.ShapeDtypeStruct((8, 8, 2 * ROWS), F32)
+    return call(slots_kernel, (block, block, stats), *args, cost=SLOTS_COST)
 
 
 def grad_kernel(
-    live_ref, kv_ref, q_ref, g_ref, st_ref, at_ref,
+    kv_ref, q_ref, g_ref, st_ref, at_ref,
     dkv_hbm, d0_ref, d1_ref, d2_ref, d3_ref, d4_ref, dx_ref,
-    kt_s, dk_acc, dv_acc, dqt_s, out_s, sems,
+    live_ref, kt_s, dk_acc, dv_acc, dqt_s, out_s, sems,
 ):
+    flags = pltpu.make_async_copy(at_ref.at[8], live_ref, sems.at[2])
+    flags.start()
     row = lax.broadcasted_iota(jnp.int32, (RUN, 1), 0)
     dqt_s[...] = jnp.zeros_like(dqt_s)
     stores = []
@@ -204,10 +252,12 @@
         kt_s[...] = kv_ref[8 * t : 8 * t + 8, 0:128, :].reshape(RUN, WIDTH).T
         dk_acc[...] = jnp.zeros_like(dk_acc)
         dv_acc[...] = jnp.zeros_like(dv_acc)
-        b = live_ref[16] + t * TILE
+        if t == 0:
+            flags.wait()
+        b = live_ref[0, 16] + t * TILE
 
         def slot_step(s, carry):
-            @pl.when(live_ref[8 * t + s] == 1)
+            @pl.when(live_ref[0, 8 * t + s] == 1)
             def _unit():
                 q = q_ref[s]
                 g = g_ref[s]
@@ -259,15 +309,15 @@
         grad_kernel,
         (KV, ONE, TWO, TWO, TWO, ONE, jax.ShapeDtypeStruct((8, WIDTH, ROWS), BF)),
         *args,
-        smem=1,
         out_specs=(pl.BlockSpec(memory_space=pl.ANY),) + (vmem,) * 6,
         scratch=[
+            pltpu.SMEM((8, 2 * ROWS), jnp.int32),
             pltpu.VMEM((WIDTH, RUN), BF),
             pltpu.VMEM((RUN, WIDTH), F32),
             pltpu.VMEM((RUN, WIDTH), F32),
             pltpu.VMEM((8, WIDTH, 2 * ROWS), F32),
             pltpu.VMEM((16, 2 * ROWS, WIDTH), BF),
-            pltpu.SemaphoreType.DMA((2,)),
+            pltpu.SemaphoreType.DMA((3,)),
         ],
     )
 
@@ -297,30 +347,25 @@
 def on_device(
     queries, key_rows, value_rows, outputs, out_grad, log_sums, doc_lengths, tile_allowed
 ):
-    z, yh, c = lax.axis_index("z"), lax.axis_index("yh"), lax.axis_index("c")
-    off = (lax.axis_index("x") * 2 + lax.axis_index("yl")) * ROWS
-    where = jnp.stack([z, yh, c, off]).astype(jnp.int32)
-
     def swap(x):
         return lax.ppermute(x, "c", [(0, 1), (1, 0)])
 
     def along_z(x, k, both_ways=True, back=False):
         return lax.ppermute(x, AXES, pairs_along_z(k, both_ways, back))
 
-    own, kv_out = prep(
-        queries, out_grad, outputs, log_sums.reshape(1, ROWS), key_rows, value_rows
-    )
+    own, at = prep(
+        queries, out_grad, outputs, log_sums.reshape(1, ROWS), doc_lengths, tile_allowed
+    )
+    own_x = swap(own)
+    kv_out = spread(key_rows, value_rows)
     kv = lax.all_to_all(kv_out, PLANE, 0, 0, tiled=True)
-    own_x = swap(own)
-    both = jnp.stack([own, own_x])
+    both = stack(own, own_x, kv_out)
     mine = [along_z(both, k, back=True) for k in (1, 2, 3)]
     mine.append(along_z(own, 4, both_ways=False, back=True))
     theirs = [swap(m) for m in mine]
 
-    q, g, stats, at, live = slots(
-        where, doc_lengths, tile_allowed, own, own_x, *mine, *theirs
-    )
-    dkv, d0, d1, d2, d3, d4, dx = grads(live, kv, q, g, stats, at)
+    q, g, stats = slots(own, own_x, *mine, *theirs)
+    dkv, d0, d1, d2, d3, d4, dx = grads(kv, q, g, stats, at)
     dkv_all = lax.all_to_all(dkv, PLANE, 0, 0, tiled=True)
     s0, s1, s2, s3, s4 = call(
         pair_kernel, (ONE, TWO, TWO, TWO, ONE), d0, d1, d2, d3, d4, swap(dx), cost=PAIR_COST

time: 67.8 us -> 64.6 us (0.953)
  the two profiles are of different devices: /device:TPU:32 before, /device:TPU:64 now
where the time goes in v1:
time: 64.6 us; the launch traced here: 64.5 us
  starting transfers between devices  27.9 us (43%)
  waiting for transfers between devices  23.1 us (36%)
  Pallas kernels  12.7 us (20%)
  between operations  0.84 us (1%)
    ppermute x8, starting transfers between devices, along_z(): return lax.ppermute(x, AXES, pairs_along_z(k, both_ways, back))  17.6 us
    ppermute x8, waiting for transfers between devices, along_z(): return lax.ppermute(x, AXES, pairs_along_z(k, both_ways, back))  11 us
    pallas_call x5, Pallas kernels, call(): pl.pallas_call(body, out_shape=out_shape, in_specs=specs, **{} if out_spe...  8.62 us
    all_to_all x1, waiting for transfers between devices, on_device(): dkv_all = lax.all_to_all(dkv, PLANE, 0, 0, tiled=True)  6.65 us
    all_to_all x1, starting transfers between devices, on_device(): kv = lax.all_to_all(kv_out, PLANE, 0, 0, tiled=True)  5.67 us
    all_to_all x1, starting transfers between devices, on_device(): dkv_all = lax.all_to_all(dkv, PLANE, 0, 0, tiled=True)  3.66 us
    all_to_all x1, waiting for transfers between devices, on_device(): kv = lax.all_to_all(kv_out, PLANE, 0, 0, tiled=True)  3.04 us
    ppermute x7, waiting for transfers between devices, swap(): return lax.ppermute(x, 'c', [(0, 1), (1, 0)])  2.46 us
  transfers between devices with their start and end apart: 17, of which 7 were waited for; matrix products, arithmetic and copies ran while one was open for 0% of the time, Pallas kernels for 3%

profile of v1, /device:TPU:64, one launch (start us, length us, event | category | flops | bytes accessed | tf_op | source)
XLA Modules:
  0.0 64.5 jit_solution(13328837757909252497)
XLA Ops:
  0.6 1.9 %shard_map.104 = (bf16[272,128]{1,0:T(8,128)(2,1)}, s32[9,8,256]{2,1,0:T(8,128)}) custom-call(bf16[128,128]{1,0:T(8,128)(2,1)} %q_hbm.1, bf16[128,128]{1,0:T(8,128)(2,1)} %g_hbm.1, bf16[128,128]{1,0:T(8,128)(2,1)} %o_hbm.1, f32[1,128]{1,0:T(1,128)} %bitcast.1, s32[16]{0:T(128)} %len_hbm.1, s32[16,16]{1,0:T(8,128)} %allow_hbm.1), custom_call_target="tpu_custom_call" | custom-call | tf_op jit(solution)/shard_map/pallas_call | solution.py:140
  2.5 0.0 copy-start.1
  2.5 0.1 collective-permute-start
  2.6 1.9 %shard_map.103.after = bf16[16,256,128]{2,1,0:T(8,128)(2,1)} custom-call(bf16[128,128]{1,0:T(8,128)(2,1)} %k_hbm.1, bf16[128,128]{1,0:T(8,128)(2,1)} %v_hbm.1), custom_call_target="tpu_custom_call" | custom-call | flops 1000000000 | bytes 2097152 | tf_op jit(solution)/shard_map/pallas_call | solution.py:176
  4.6 0.0 collective-permute-done.other_ref.own_x_ref
  4.6 0.0 copy-done.1
  4.6 0.2 shard_map.105
  4.8 1.3 %collective-permute-start.3 = (bf16[2,272,128]{2,1,0:T(8,128)(2,1)S(1)}, bf16[2,272,128]{2,1,0:T(8,128)(2,1)S(1)}, u32[]{:S(2)}, u32[]{:S(2)}) collective-permute-start(bf16[2,272,128]{2,1,0:T(8,128)(2,1)S(1)} %shard_map.105), channel_id=1, source_target_pairs={{96,0},{97,1},{98,2},{99,3},{100,4},{101,5},{102,6},{103,7},{168,8... | collective-permute-start | bytes 417800 | tf_op jit(solution)/shard_map/ppermute | solution.py:354
  6.1 3.3 %collective-permute-start.2 = (bf16[2,272,128]{2,1,0:T(8,128)(2,1)S(1)}, bf16[2,272,128]{2,1,0:T(8,128)(2,1)S(1)}, u32[]{:S(2)}, u32[]{:S(2)}) collective-permute-start(bf16[2,272,128]{2,1,0:T(8,128)(2,1)S(1)} %shard_map.105), channel_id=1, source_target_pairs={{64,0},{65,1},{66,2},{67,3},{68,4},{69,5},{70,6},{71,7},{200,8},{2... | collective-permute-start | bytes 417800 | tf_op jit(solution)/shard_map/ppermute | solution.py:354
  9.4 1.9 %collective-permute-start.1 = (bf16[2,272,128]{2,1,0:T(8,128)(2,1)S(1)}, bf16[2,272,128]{2,1,0:T(8,128)(2,1)S(1)}, u32[]{:S(2)}, u32[]{:S(2)}) collective-permute-start(bf16[2,272,128]{2,1,0:T(8,128)(2,1)S(1)} %shard_map.105), channel_id=1, source_target_pairs={{32,0},{33,1},{34,2},{35,3},{36,4},{37,5},{38,6},{39,7},{232,8},{2... | collective-permute-start | bytes 417800 | tf_op jit(solution)/shard_map/ppermute | solution.py:354
  11.4 5.7 %all-to-all-start = ((bf16[16,256,128]{2,1,0:T(8,128)(2,1)}), bf16[16,256,128]{2,1,0:T(8,128)(2,1)S(1)}, u32[]{:S(2)}, u32[]{:S(2)}) async-start(bf16[16,256,128]{2,1,0:T(8,128)(2,1)} %shard_map.103.after), calls=%async_computation | async-start | bytes 2097152 | tf_op jit(solution)/shard_map/all_to_all | solution.py:361
  17.0 0.0 copy-start
  17.0 1.4 %collective-permute-start.4 = (bf16[272,128]{1,0:T(8,128)(2,1)S(1)}, bf16[272,128]{1,0:T(8,128)(2,1)S(1)}, u32[]{:S(2)}, u32[]{:S(2)}) collective-permute-start(bf16[272,128]{1,0:T(8,128)(2,1)S(1)} %copy-done.1), channel_id=1, source_target_pairs={{128,0},{129,1},{130,2},{131,3},{132,4},{133,5},{134,6},{135,7},{1... | collective-permute-start | bytes 208904 | tf_op jit(solution)/shard_map/ppermute | solution.py:354
  18.5 0.0 collective-permute-done.3.m3_ref
  18.5 0.1 collective-permute-start.7
  18.6 1.6 %collective-permute-done.2.m2_ref = bf16[2,272,128]{2,1,0:T(8,128)(2,1)S(1)} collective-permute-done((bf16[2,272,128]{2,1,0:T(8,128)(2,1)S(1)}, bf16[2,272,128]{2,1,0:T(8,128)(2,1)S(1)}, u32[]{:S(2)}, u32[]{:S(2)}) %collective-permute-start.2) | collective-permute-done | bytes 139296 | tf_op jit(solution)/shard_map/ppermute | solution.py:354
  20.2 0.0 collective-permute-start.6
  20.2 0.0 collective-permute-done.1.m1_ref
  20.3 0.5 collective-permute-start.5
  20.8 7.7 %collective-permute-done.4.m4_ref = bf16[272,128]{1,0:T(8,128)(2,1)S(1)} collective-permute-done((bf16[272,128]{1,0:T(8,128)(2,1)S(1)}, bf16[272,128]{1,0:T(8,128)(2,1)S(1)}, u32[]{:S(2)}, u32[]{:S(2)}) %collective-permute-start.4) | collective-permute-done | bytes 69664 | tf_op jit(solution)/shard_map/ppermute | solution.py:354
  28.5 0.0 collective-permute-start.8
  28.5 1.3 %collective-permute-done.8.x4_ref = bf16[272,128]{1,0:T(8,128)(2,1)S(1)} collective-permute-done((bf16[272,128]{1,0:T(8,128)(2,1)S(1)}, bf16[272,128]{1,0:T(8,128)(2,1)S(1)}, u32[]{:S(2)}, u32[]{:S(2)}) %collective-permute-start.8) | collective-permute-done | bytes 69664 | tf_op jit(solution)/shard_map/ppermute | solution.py:351
  29.8 0.0 collective-permute-done.7.x3_ref
  29.8 0.0 collective-permute-done.6.x2_ref
  29.8 0.0 collective-permute-done.5.x1_ref
  29.8 0.1 shard_map.106
  29.9 3.0 %all-to-all-done.kv_ref = bf16[16,256,128]{2,1,0:T(8,128)(2,1)S(1)} async-done(((bf16[16,256,128]{2,1,0:T(8,128)(2,1)}), bf16[16,256,128]{2,1,0:T(8,128)(2,1)S(1)}, u32[]{:S(2)}, u32[]{:S(2)}) %all-to-all-start) | async-done | bytes 1048608 | tf_op jit(solution)/shard_map/all_to_all | solution.py:361
  32.9 0.0 copy-done
  32.9 7.7 %shard_map.107 = (bf16[16,256,128]{2,1,0:T(8,128)(2,1)}, bf16[128,128]{1,0:T(8,128)(2,1)S(1)}, bf16[2,128,128]{2,1,0:T(8,128)(2,1)S(1)}, bf16[2,128,128]{2,1,0:T...) custom-call(bf16[16,256,128]{2,1,0:T(8,128)(2,1)S(1)} %all-to-all-do, ...), custom_call_target="tpu_custom_call" | custom-call | tf_op jit(solution)/shard_map/pallas_call | solution.py:46
  40.6 0.1 collective-permute-start.9
  40.7 3.7 %all-to-all-start.1 = ((bf16[16,256,128]{2,1,0:T(8,128)(2,1)}), bf16[16,256,128]{2,1,0:T(8,128)(2,1)S(1)}, u32[]{:S(2)}, u32[]{:S(2)}) async-start(bf16[16,256,128]{2,1,0:T(8,128)(2,1)} %get-tuple-element.27), calls=%async_computation.1 | async-start | bytes 2097152 | tf_op jit(solution)/shard_map/all_to_all | solution.py:369
  44.3 0.0 collective-permute-done.9.got
  44.4 0.1 shard_map.108
  44.4 1.9 %collective-permute-start.10 = (bf16[2,128,128]{2,1,0:T(8,128)(2,1)S(1)}, bf16[2,128,128]{2,1,0:T(8,128)(2,1)S(1)}, u32[]{:S(2)}, u32[]{:S(2)}) collective-permute-start(bf16[2,128,128]{2,1,0:T(8,128)(2,1)S(1)} %get-tuple-element.35), channel_id=1, source_target_pairs={{0,32},{1,33},{2,34},{3,35},{4,36},{5,37},{6,38},{7,39},{8,232},{9... | collective-permute-start | bytes 196616 | tf_op jit(solution)/shard_map/ppermute | solution.py:354
  46.4 5.0 %collective-permute-start.11 = (bf16[2,128,128]{2,1,0:T(8,128)(2,1)S(1)}, bf16[2,128,128]{2,1,0:T(8,128)(2,1)S(1)}, u32[]{:S(2)}, u32[]{:S(2)}) collective-permute-start(bf16[2,128,128]{2,1,0:T(8,128)(2,1)S(1)} %get-tuple-element.36), channel_id=1, source_target_pairs={{0,64},{1,65},{2,66},{3,67},{4,68},{5,69},{6,70},{7,71},{8,200},{9... | collective-permute-start | bytes 196616 | tf_op jit(solution)/shard_map/ppermute | solution.py:354
  51.4 1.5 %collective-permute-start.12 = (bf16[2,128,128]{2,1,0:T(8,128)(2,1)S(1)}, bf16[2,128,128]{2,1,0:T(8,128)(2,1)S(1)}, u32[]{:S(2)}, u32[]{:S(2)}) collective-permute-start(bf16[2,128,128]{2,1,0:T(8,128)(2,1)S(1)} %get-tuple-element.37), channel_id=1, source_target_pairs={{0,96},{1,97},{2,98},{3,99},{4,100},{5,101},{6,102},{7,103},{8,168... | collective-permute-start | bytes 196616 | tf_op jit(solution)/shard_map/ppermute | solution.py:354
  52.9 1.3 %collective-permute-start.13 = (bf16[128,128]{1,0:T(8,128)(2,1)S(1)}, bf16[128,128]{1,0:T(8,128)(2,1)S(1)}, u32[]{:S(2)}, u32[]{:S(2)}) collective-permute-start(bf16[128,128]{1,0:T(8,128)(2,1)S(1)} %get-tuple-element.38), channel_id=1, source_target_pairs={{0,128},{1,129},{2,130},{3,131},{4,132},{5,133},{6,134},{7,135},{8... | collective-permute-start | bytes 98312 | tf_op jit(solution)/shard_map/ppermute | solution.py:354
  54.2 1.6 %collective-permute-done.13.e4 = bf16[128,128]{1,0:T(8,128)(2,1)S(1)} collective-permute-done((bf16[128,128]{1,0:T(8,128)(2,1)S(1)}, bf16[128,128]{1,0:T(8,128)(2,1)S(1)}, u32[]{:S(2)}, u32[]{:S(2)}) %collective-permute-start.13) | collective-permute-done | bytes 32800 | tf_op jit(solution)/shard_map/ppermute | solution.py:354
  55.7 0.0 collective-permute-done.10.e1
  55.8 0.0 collective-permute-done.11.e2
  55.8 0.0 collective-permute-done.12.e3
  55.8 0.1 collective-permute-start.14
  55.9 1.2 %collective-permute-done.14.got = bf16[128,128]{1,0:T(8,128)(2,1)S(1)} collective-permute-done((bf16[128,128]{1,0:T(8,128)(2,1)S(1)}, bf16[128,128]{1,0:T(8,128)(2,1)S(1)}, u32[]{:S(2)}, u32[]{:S(2)}) %collective-permute-start.14) | collective-permute-done | bytes 32800 | tf_op jit(solution)/shard_map/ppermute | solution.py:351
  57.1 6.6 %all-to-all-done.1.dkv_all = bf16[16,256,128]{2,1,0:T(8,128)(2,1)S(1)} async-done(((bf16[16,256,128]{2,1,0:T(8,128)(2,1)}), bf16[16,256,128]{2,1,0:T(8,128)(2,1)S(1)}, u32[]{:S(2)}, u32[]{:S(2)}) %all-to-all-start.1) | async-done | bytes 1048608 | tf_op jit(solution)/shard_map/all_to_all | solution.py:369
  63.7 0.8 %shard_map.110 = (bf16[128,128]{1,0:T(8,128)(2,1)}, bf16[128,128]{1,0:T(8,128)(2,1)}, bf16[128,128]{1,0:T(8,128)(2,1)}) custom-call(bf16[16,256,128]{2,1,0:T(8,128)(2,1)S(1)} %all-to-all-done.1.dkv_all, f32[128,128]{1,0:T(8,128)S(1)} %get-tuple-element.39.keep, bf16[128,128]{1,0:T(8,128)(2,1)S(1)} %collective-permute-done.14.got), custom_call_target="tpu_custom_call" | custom-call | tf_op jit(solution)/shard_map/pallas_call | solution.py:46
  (1 shorter events, 0.0 us)
Async XLA Ops:
  2.5 2.1 %copy-start.1 = (bf16[272,128]{1,0:T(8,128)(2,1)S(1)}, bf16[272,128]{1,0:T(8,128)(2,1)}, u32[]{:S(2)}) copy-start(bf16[272,128]{1,0:T(8,128)(2,1)} %get-tuple-element.22.own_ref) | copy-start | bytes 208900
  2.5 2.0 %collective-permute-start = (bf16[272,128]{1,0:T(8,128)(2,1)}, bf16[272,128]{1,0:T(8,128)(2,1)S(1)}, u32[]{:S(2)}, u32[]{:S(2)}) collective-permute-start(bf16[272,128]{1,0:T(8,128)(2,1)} %get-tuple-element.22.own_ref), channel_id=1, source_target_pairs={{0,8},{8,0},{1,9},{9,1},{2,10},{10,2},{3,11},{11,3},{4,12},{12,4},... | collective-permute-start | bytes 208904 | tf_op jit(solution)/shard_map/ppermute | solution.py:351
  4.8 13.7 %collective-permute-start.3 = (bf16[2,272,128]{2,1,0:T(8,128)(2,1)S(1)}, bf16[2,272,128]{2,1,0:T(8,128)(2,1)S(1)}, u32[]{:S(2)}, u32[]{:S(2)}) collective-permute-start(bf16[2,272,128]{2,1,0:T(8,128)(2,1)S(1)} %shard_map.105), channel_id=1, source_target_pairs={{96,0},{97,1},{98,2},{99,3},{100,4},{101,5},{102,6},{103,7},{168,8... | collective-permute-start | bytes 417800 | tf_op jit(solution)/shard_map/ppermute | solution.py:354
  6.1 14.1 %collective-permute-start.2 = (bf16[2,272,128]{2,1,0:T(8,128)(2,1)S(1)}, bf16[2,272,128]{2,1,0:T(8,128)(2,1)S(1)}, u32[]{:S(2)}, u32[]{:S(2)}) collective-permute-start(bf16[2,272,128]{2,1,0:T(8,128)(2,1)S(1)} %shard_map.105), channel_id=1, source_target_pairs={{64,0},{65,1},{66,2},{67,3},{68,4},{69,5},{70,6},{71,7},{200,8},{2... | collective-permute-start | bytes 417800 | tf_op jit(solution)/shard_map/ppermute | solution.py:354
  9.4 10.8 %collective-permute-start.1 = (bf16[2,272,128]{2,1,0:T(8,128)(2,1)S(1)}, bf16[2,272,128]{2,1,0:T(8,128)(2,1)S(1)}, u32[]{:S(2)}, u32[]{:S(2)}) collective-permute-start(bf16[2,272,128]{2,1,0:T(8,128)(2,1)S(1)} %shard_map.105), channel_id=1, source_target_pairs={{32,0},{33,1},{34,2},{35,3},{36,4},{37,5},{38,6},{39,7},{232,8},{2... | collective-permute-start | bytes 417800 | tf_op jit(solution)/shard_map/ppermute | solution.py:354
  11.4 21.5 %all-to-all-start = ((bf16[16,256,128]{2,1,0:T(8,128)(2,1)}), bf16[16,256,128]{2,1,0:T(8,128)(2,1)S(1)}, u32[]{:S(2)}, u32[]{:S(2)}) async-start(bf16[16,256,128]{2,1,0:T(8,128)(2,1)} %shard_map.103.after), calls=%async_computation | async-start | bytes 2097152 | tf_op jit(solution)/shard_map/all_to_all | solution.py:361
  17.0 15.9 %copy-start = (s32[9,8,256]{2,1,0:T(8,128)S(1)}, s32[9,8,256]{2,1,0:T(8,128)}, u32[]{:S(2)}) copy-start(s32[9,8,256]{2,1,0:T(8,128)} %get-tuple-element.26.at_ref) | copy-start | bytes 221188
  17.0 11.4 %collective-permute-start.4 = (bf16[272,128]{1,0:T(8,128)(2,1)S(1)}, bf16[272,128]{1,0:T(8,128)(2,1)S(1)}, u32[]{:S(2)}, u32[]{:S(2)}) collective-permute-start(bf16[272,128]{1,0:T(8,128)(2,1)S(1)} %copy-done.1), channel_id=1, source_target_pairs={{128,0},{129,1},{130,2},{131,3},{132,4},{133,5},{134,6},{135,7},{1... | collective-permute-start | bytes 208904 | tf_op jit(solution)/shard_map/ppermute | solution.py:354
  18.5 11.3 %collective-permute-start.7 = (bf16[2,272,128]{2,1,0:T(8,128)(2,1)S(1)}, bf16[2,272,128]{2,1,0:T(8,128)(2,1)S(1)}, u32[]{:S(2)}, u32[]{:S(2)}) collective-permute-start(bf16[2,272,128]{2,1,0:T(8,128)(2,1)S(1)} %collective-permute-done.3.m3_ref), channel_id=1, source_target_pairs={{0,8},{8,0},{1,9},{9,1},{2,10},{10,2},{3,11},{11,3},{4,12},{12,4},... | collective-permute-start | bytes 417800 | tf_op jit(solution)/shard_map/ppermute | solution.py:351
  20.2 9.5 %collective-permute-start.6 = (bf16[2,272,128]{2,1,0:T(8,128)(2,1)S(1)}, bf16[2,272,128]{2,1,0:T(8,128)(2,1)S(1)}, u32[]{:S(2)}, u32[]{:S(2)}) collective-permute-start(bf16[2,272,128]{2,1,0:T(8,128)(2,1)S(1)} %collective-permute-done.2.m2_ref), channel_id=1, source_target_pairs={{0,8},{8,0},{1,9},{9,1},{2,10},{10,2},{3,11},{11,3},{4,12},{12,4},... | collective-permute-start | bytes 417800 | tf_op jit(solution)/shard_map/ppermute | solution.py:351
  20.3 9.5 %collective-permute-start.5 = (bf16[2,272,128]{2,1,0:T(8,128)(2,1)S(1)}, bf16[2,272,128]{2,1,0:T(8,128)(2,1)S(1)}, u32[]{:S(2)}, u32[]{:S(2)}) collective-permute-start(bf16[2,272,128]{2,1,0:T(8,128)(2,1)S(1)} %collective-permute-done.1.m1_ref), channel_id=1, source_target_pairs={{0,8},{8,0},{1,9},{9,1},{2,10},{10,2},{3,11},{11,3},{4,12},{12,4},... | collective-permute-start | bytes 417800 | tf_op jit(solution)/shard_map/ppermute | solution.py:351
  28.5 1.3 %collective-permute-start.8 = (bf16[272,128]{1,0:T(8,128)(2,1)S(1)}, bf16[272,128]{1,0:T(8,128)(2,1)S(1)}, u32[]{:S(2)}, u32[]{:S(2)}) collective-permute-start(bf16[272,128]{1,0:T(8,128)(2,1)S(1)} %collective-permute-done.4.m4_ref), channel_id=1, source_target_pairs={{0,8},{8,0},{1,9},{9,1},{2,10},{10,2},{3,11},{11,3},{4,12},{12,4},... | collective-permute-start | bytes 208904 | tf_op jit(solution)/shard_map/ppermute | solution.py:351
  40.6 3.8 %collective-permute-start.9 = (bf16[8,128,128]{2,1,0:T(8,128)(2,1)S(1)}, bf16[8,128,128]{2,1,0:T(8,128)(2,1)S(1)}, u32[]{:S(2)}, u32[]{:S(2)}) collective-permute-start(bf16[8,128,128]{2,1,0:T(8,128)(2,1)S(1)} %get-tuple-element.33), channel_id=1, source_target_pairs={{0,8},{8,0},{1,9},{9,1},{2,10},{10,2},{3,11},{11,3},{4,12},{12,4},... | collective-permute-start | bytes 786440 | tf_op jit(solution)/shard_map/ppermute | solution.py:351
  40.7 23.1 %all-to-all-start.1 = ((bf16[16,256,128]{2,1,0:T(8,128)(2,1)}), bf16[16,256,128]{2,1,0:T(8,128)(2,1)S(1)}, u32[]{:S(2)}, u32[]{:S(2)}) async-start(bf16[16,256,128]{2,1,0:T(8,128)(2,1)} %get-tuple-element.27), calls=%async_computation.1 | async-start | bytes 2097152 | tf_op jit(solution)/shard_map/all_to_all | solution.py:369
  44.4 11.3 %collective-permute-start.10 = (bf16[2,128,128]{2,1,0:T(8,128)(2,1)S(1)}, bf16[2,128,128]{2,1,0:T(8,128)(2,1)S(1)}, u32[]{:S(2)}, u32[]{:S(2)}) collective-permute-start(bf16[2,128,128]{2,1,0:T(8,128)(2,1)S(1)} %get-tuple-element.35), channel_id=1, source_target_pairs={{0,32},{1,33},{2,34},{3,35},{4,36},{5,37},{6,38},{7,39},{8,232},{9... | collective-permute-start | bytes 196616 | tf_op jit(solution)/shard_map/ppermute | solution.py:354
  46.4 9.4 %collective-permute-start.11 = (bf16[2,128,128]{2,1,0:T(8,128)(2,1)S(1)}, bf16[2,128,128]{2,1,0:T(8,128)(2,1)S(1)}, u32[]{:S(2)}, u32[]{:S(2)}) collective-permute-start(bf16[2,128,128]{2,1,0:T(8,128)(2,1)S(1)} %get-tuple-element.36), channel_id=1, source_target_pairs={{0,64},{1,65},{2,66},{3,67},{4,68},{5,69},{6,70},{7,71},{8,200},{9... | collective-permute-start | bytes 196616 | tf_op jit(solution)/shard_map/ppermute | solution.py:354
  51.4 4.4 %collective-permute-start.12 = (bf16[2,128,128]{2,1,0:T(8,128)(2,1)S(1)}, bf16[2,128,128]{2,1,0:T(8,128)(2,1)S(1)}, u32[]{:S(2)}, u32[]{:S(2)}) collective-permute-start(bf16[2,128,128]{2,1,0:T(8,128)(2,1)S(1)} %get-tuple-element.37), channel_id=1, source_target_pairs={{0,96},{1,97},{2,98},{3,99},{4,100},{5,101},{6,102},{7,103},{8,168... | collective-permute-start | bytes 196616 | tf_op jit(solution)/shard_map/ppermute | solution.py:354
  52.9 2.9 %collective-permute-start.13 = (bf16[128,128]{1,0:T(8,128)(2,1)S(1)}, bf16[128,128]{1,0:T(8,128)(2,1)S(1)}, u32[]{:S(2)}, u32[]{:S(2)}) collective-permute-start(bf16[128,128]{1,0:T(8,128)(2,1)S(1)} %get-tuple-element.38), channel_id=1, source_target_pairs={{0,128},{1,129},{2,130},{3,131},{4,132},{5,133},{6,134},{7,135},{8... | collective-permute-start | bytes 98312 | tf_op jit(solution)/shard_map/ppermute | solution.py:354
  55.8 1.3 %collective-permute-start.14 = (bf16[128,128]{1,0:T(8,128)(2,1)S(1)}, bf16[128,128]{1,0:T(8,128)(2,1)S(1)}, u32[]{:S(2)}, u32[]{:S(2)}) collective-permute-start(bf16[128,128]{1,0:T(8,128)(2,1)S(1)} %get-tuple-element.40), channel_id=1, source_target_pairs={{0,8},{8,0},{1,9},{9,1},{2,10},{10,2},{3,11},{11,3},{4,12},{12,4},... | collective-permute-start | bytes 98312 | tf_op jit(solution)/shard_map/ppermute | solution.py:351

commit v2 on v1

--- a/solution.py
+++ b/solution.py
@@ -72,17 +72,13 @@
 
 
 def prep_kernel(
-    q_hbm, g_hbm, o_hbm, lse_hbm, len_hbm, allow_hbm,
-    pack_ref, at_ref,
-    o_s, lse_s, len_s, allow_s, sems,
+    q_hbm, g_hbm, o_hbm, lse_hbm, pack_ref, o_s, lse_s, sems
 ):
     loads = [
         pltpu.make_async_copy(g_hbm, pack_ref.at[128:256], sems.at[0]),
         pltpu.make_async_copy(o_hbm, o_s, sems.at[1]),
         pltpu.make_async_copy(lse_hbm, lse_s, sems.at[2]),
-        pltpu.make_async_copy(len_hbm, len_s, sems.at[3]),
-        pltpu.make_async_copy(allow_hbm, allow_s, sems.at[4]),
-        pltpu.make_async_copy(q_hbm, pack_ref.at[0:128], sems.at[5]),
+        pltpu.make_async_copy(q_hbm, pack_ref.at[0:128], sems.at[3]),
     ]
     for copy in loads:
         copy.start()
@@ -96,7 +92,31 @@
     pack_ref[256:272] = jnp.concatenate(stats, axis=0).astype(BF)
 
     loads[3].wait()
-    loads[4].wait()
+
+
+def prep(*args):
+    return pl.pallas_call(
+        prep_kernel,
+        out_shape=jax.ShapeDtypeStruct((PACK, WIDTH), BF),
+        in_specs=[pl.BlockSpec(memory_space=pl.ANY)] * 4,
+        out_specs=pl.BlockSpec(memory_space=pltpu.VMEM),
+        scratch_shapes=[
+            pltpu.VMEM((ROWS, WIDTH), BF),
+            pltpu.VMEM((1, ROWS), F32),
+            pltpu.SemaphoreType.DMA((4,)),
+        ],
+    )(*args)
+
+
+def plan_kernel(len_hbm, allow_hbm, after, at_ref, len_s, allow_s, sems):
+    loads = [
+        pltpu.make_async_copy(len_hbm, len_s, sems.at[0]),
+        pltpu.make_async_copy(allow_hbm, allow_s, sems.at[1]),
+    ]
+    for copy in loads:
+        copy.start()
+    for copy in loads:
+        copy.wait()
     z, yh, c = lax.axis_index("z"), lax.axis_index("yh"), lax.axis_index("c")
     off = (lax.axis_index("x") * 2 + lax.axis_index("yl")) * ROWS
     ends = []
@@ -131,27 +151,21 @@
         at_ref[s, 0:1] = start[s : s + 1]
         at_ref[s, 1:2] = pos[s : s + 1]
     at_ref[8] = live
-    loads[5].wait()
-
-
-def prep(*args):
-    hbm = pl.BlockSpec(memory_space=pl.ANY)
-    vmem = pl.BlockSpec(memory_space=pltpu.VMEM)
+
+
+def plan(*args):
     return pl.pallas_call(
-        prep_kernel,
-        out_shape=(
-            jax.ShapeDtypeStruct((PACK, WIDTH), BF),
-            jax.ShapeDtypeStruct((9, 8, 2 * ROWS), jnp.int32),
-        ),
-        in_specs=[hbm] * 6,
-        out_specs=(vmem, vmem),
+        plan_kernel,
+        out_shape=jax.ShapeDtypeStruct((9, 8, 2 * ROWS), jnp.int32),
+        in_specs=[pl.BlockSpec(memory_space=pl.ANY)] * 3,
+        out_specs=pl.BlockSpec(memory_space=pltpu.VMEM),
         scratch_shapes=[
-            pltpu.VMEM((ROWS, WIDTH), BF),
-            pltpu.VMEM((1, ROWS), F32),
             pltpu.SMEM((NDOCS,), jnp.int32),
             pltpu.SMEM((16, 16), jnp.int32),
-            pltpu.SemaphoreType.DMA((6,)),
+            pltpu.SemaphoreType.DMA((2,)),
         ],
+        cost_estimate=SPREAD_COST,
+        compiler_params=pltpu.CompilerParams(vmem_limit_bytes=32 * 1024 * 1024),
     )(*args)
 
 
@@ -353,15 +367,14 @@
     def along_z(x, k, both_ways=True, back=False):
         return lax.ppermute(x, AXES, pairs_along_z(k, both_ways, back))
 
-    own, at = prep(
-        queries, out_grad, outputs, log_sums.reshape(1, ROWS), doc_lengths, tile_allowed
-    )
+    own = prep(queries, out_grad, outputs, log_sums.reshape(1, ROWS))
     own_x = swap(own)
     kv_out = spread(key_rows, value_rows)
     kv = lax.all_to_all(kv_out, PLANE, 0, 0, tiled=True)
     both = stack(own, own_x, kv_out)
     mine = [along_z(both, k, back=True) for k in (1, 2, 3)]
     mine.append(along_z(own, 4, both_ways=False, back=True))
+    at = plan(doc_lengths, tile_allowed, mine[0])
     theirs = [swap(m) for m in mine]
 
     q, g, stats = slots(own, own_x, *mine, *theirs)

time: 64.6 us -> 65.4 us (1.012)
  the two profiles are of different devices: /device:TPU:64 before, /device:TPU:32 now
where the time goes in v2:
time: 65.4 us; the launch traced here: 64.2 us
  starting transfers between devices  30.4 us (46%)
  waiting for transfers between devices  20.4 us (31%)
  Pallas kernels  12.4 us (19%)
  between operations  0.85 us (1%)
    ppermute x8, starting transfers between devices, along_z(): return lax.ppermute(x, AXES, pairs_along_z(k, both_ways, back))  19.1 us
    ppermute x8, waiting for transfers between devices, along_z(): return lax.ppermute(x, AXES, pairs_along_z(k, both_ways, back))  11.1 us
    pallas_call x5, Pallas kernels, call(): pl.pallas_call(body, out_shape=out_shape, in_specs=specs, **{} if out_spe...  7.8 us
    all_to_all x1, starting transfers between devices, on_device(): kv = lax.all_to_all(kv_out, PLANE, 0, 0, tiled=True)  5.31 us
    all_to_all x1, starting transfers between devices, on_device(): dkv_all = lax.all_to_all(dkv, PLANE, 0, 0, tiled=True)  4.59 us
    all_to_all x1, waiting for transfers between devices, on_device(): dkv_all = lax.all_to_all(dkv, PLANE, 0, 0, tiled=True)  4.11 us
    all_to_all x1, waiting for transfers between devices, on_device(): kv = lax.all_to_all(kv_out, PLANE, 0, 0, tiled=True)  3.66 us
    pallas_call x1, Pallas kernels, spread(): pl.pallas_call(spread_kernel, out_shape=KV, in_specs=[hbm] * 2, out_specs...  1.94 us
  transfers between devices with their start and end apart: 17, of which 8 were waited for; matrix products, arithmetic and copies ran while one was open for 0% of the time, Pallas kernels for 5%

profile of v2, /device:TPU:32, one launch (start us, length us, event | category | flops | bytes accessed | tf_op | source)
XLA Modules:
  0.0 64.2 jit_solution(16050775277034803804)
XLA Ops:
  0.6 1.6 %shard_map.104.own_ref = bf16[272,128]{1,0:T(8,128)(2,1)} custom-call(bf16[128,128]{1,0:T(8,128)(2,1)} %q_hbm.1, bf16[128,128]{1,0:T(8,128)(2,1)} %g_hbm.1, bf16[128,128]{1,0:T(8,128)(2,1)} %o_hbm.1, f32[1,128]{1,0:T(1,128)} %bitcast.1), custom_call_target="tpu_custom_call" | custom-call | tf_op jit(solution)/shard_map/pallas_call | solution.py:98
  2.2 0.0 copy-start
  2.2 0.1 collective-permute-start
  2.3 1.9 %shard_map.103.after = bf16[16,256,128]{2,1,0:T(8,128)(2,1)} custom-call(bf16[128,128]{1,0:T(8,128)(2,1)} %k_hbm.1, bf16[128,128]{1,0:T(8,128)(2,1)} %v_hbm.1), custom_call_target="tpu_custom_call" | custom-call | flops 1000000000 | bytes 2097152 | tf_op jit(solution)/shard_map/pallas_call | solution.py:190
  4.2 0.0 collective-permute-done.other_ref.own_x_ref
  4.3 0.0 copy-done
  4.3 0.2 shard_map.105
  4.5 0.0 copy-start.1
  4.5 0.0 copy-start.2
  4.5 1.3 %collective-permute-start.3 = (bf16[2,272,128]{2,1,0:T(8,128)(2,1)S(1)}, bf16[2,272,128]{2,1,0:T(8,128)(2,1)S(1)}, u32[]{:S(2)}, u32[]{:S(2)}) collective-permute-start(bf16[2,272,128]{2,1,0:T(8,128)(2,1)S(1)} %shard_map.105), channel_id=1, source_target_pairs={{96,0},{97,1},{98,2},{99,3},{100,4},{101,5},{102,6},{103,7},{168,8... | collective-permute-start | bytes 417800 | tf_op jit(solution)/shard_map/ppermute | solution.py:368
  5.8 1.3 %collective-permute-start.2 = (bf16[2,272,128]{2,1,0:T(8,128)(2,1)S(1)}, bf16[2,272,128]{2,1,0:T(8,128)(2,1)S(1)}, u32[]{:S(2)}, u32[]{:S(2)}) collective-permute-start(bf16[2,272,128]{2,1,0:T(8,128)(2,1)S(1)} %shard_map.105), channel_id=1, source_target_pairs={{64,0},{65,1},{66,2},{67,3},{68,4},{69,5},{70,6},{71,7},{200,8},{2... | collective-permute-start | bytes 417800 | tf_op jit(solution)/shard_map/ppermute | solution.py:368
  7.1 3.8 %collective-permute-start.1 = (bf16[2,272,128]{2,1,0:T(8,128)(2,1)S(1)}, bf16[2,272,128]{2,1,0:T(8,128)(2,1)S(1)}, u32[]{:S(2)}, u32[]{:S(2)}) collective-permute-start(bf16[2,272,128]{2,1,0:T(8,128)(2,1)S(1)} %shard_map.105), channel_id=1, source_target_pairs={{32,0},{33,1},{34,2},{35,3},{36,4},{37,5},{38,6},{39,7},{232,8},{2... | collective-permute-start | bytes 417800 | tf_op jit(solution)/shard_map/ppermute | solution.py:368
  10.9 5.3 %all-to-all-start = ((bf16[16,256,128]{2,1,0:T(8,128)(2,1)}), bf16[16,256,128]{2,1,0:T(8,128)(2,1)S(1)}, u32[]{:S(2)}, u32[]{:S(2)}) async-start(bf16[16,256,128]{2,1,0:T(8,128)(2,1)} %shard_map.103.after), calls=%async_computation | async-start | bytes 2097152 | tf_op jit(solution)/shard_map/all_to_all | solution.py:373
  16.2 1.3 %collective-permute-start.4 = (bf16[272,128]{1,0:T(8,128)(2,1)S(1)}, bf16[272,128]{1,0:T(8,128)(2,1)S(1)}, u32[]{:S(2)}, u32[]{:S(2)}) collective-permute-start(bf16[272,128]{1,0:T(8,128)(2,1)S(1)} %copy-done), channel_id=1, source_target_pairs={{128,0},{129,1},{130,2},{131,3},{132,4},{133,5},{134,6},{135,7},{1... | collective-permute-start | bytes 208904 | tf_op jit(solution)/shard_map/ppermute | solution.py:368
  17.5 0.8 %collective-permute-done.3.m3_ref = bf16[2,272,128]{2,1,0:T(8,128)(2,1)S(1)} collective-permute-done((bf16[2,272,128]{2,1,0:T(8,128)(2,1)S(1)}, bf16[2,272,128]{2,1,0:T(8,128)(2,1)S(1)}, u32[]{:S(2)}, u32[]{:S(2)}) %collective-permute-start.3) | collective-permute-done | bytes 139296 | tf_op jit(solution)/shard_map/ppermute | solution.py:368
  18.3 0.0 collective-permute-start.7
  18.3 0.8 %collective-permute-done.2.m2_ref = bf16[2,272,128]{2,1,0:T(8,128)(2,1)S(1)} collective-permute-done((bf16[2,272,128]{2,1,0:T(8,128)(2,1)S(1)}, bf16[2,272,128]{2,1,0:T(8,128)(2,1)S(1)}, u32[]{:S(2)}, u32[]{:S(2)}) %collective-permute-start.2) | collective-permute-done | bytes 139296 | tf_op jit(solution)/shard_map/ppermute | solution.py:368
  19.1 1.1 %collective-permute-start.6 = (bf16[2,272,128]{2,1,0:T(8,128)(2,1)S(1)}, bf16[2,272,128]{2,1,0:T(8,128)(2,1)S(1)}, u32[]{:S(2)}, u32[]{:S(2)}) collective-permute-start(bf16[2,272,128]{2,1,0:T(8,128)(2,1)S(1)} %collective-permute-done.2.m2_ref), channel_id=1, source_target_pairs={{0,8},{8,0},{1,9},{9,1},{2,10},{10,2},{3,11},{11,3},{4,12},{12,4},... | collective-permute-start | bytes 417800 | tf_op jit(solution)/shard_map/ppermute | solution.py:365
  20.2 0.0 collective-permute-done.1.m1_ref.after
  20.2 0.0 collective-permute-start.5
  20.2 8.0 %collective-permute-done.4.m4_ref = bf16[272,128]{1,0:T(8,128)(2,1)S(1)} collective-permute-done((bf16[272,128]{1,0:T(8,128)(2,1)S(1)}, bf16[272,128]{1,0:T(8,128)(2,1)S(1)}, u32[]{:S(2)}, u32[]{:S(2)}) %collective-permute-start.4) | collective-permute-done | bytes 69664 | tf_op jit(solution)/shard_map/ppermute | solution.py:368
  28.2 0.0 collective-permute-start.8
  28.2 0.0 copy-done.1
  28.2 0.0 copy-done.2
  28.2 0.9 %shard_map.107.at_ref = s32[9,8,256]{2,1,0:T(8,128)S(1)} custom-call(s32[16]{0:T(128)S(1)} %copy-done.2, s32[16,16]{1,0:T(8,128)S(1)} %copy-done.1, bf16[2,272,128]{2,1,0:T(8,128)(2,1)S(1)} %collective-permute-done.1.m1_ref.after), custom_call_target="tpu_custom_call" | custom-call | flops 1000000000 | bytes 2097152 | tf_op jit(solution)/shard_map/pallas_call | solution.py:157
  29.1 0.3 collective-permute-done.8.x4_ref
  29.5 0.0 collective-permute-done.7.x3_ref
  29.5 0.0 collective-permute-done.6.x2_ref
  29.5 0.0 collective-permute-done.5.x1_ref
  29.5 0.1 shard_map.106
  29.6 3.7 %all-to-all-done.kv_ref = bf16[16,256,128]{2,1,0:T(8,128)(2,1)S(1)} async-done(((bf16[16,256,128]{2,1,0:T(8,128)(2,1)}), bf16[16,256,128]{2,1,0:T(8,128)(2,1)S(1)}, u32[]{:S(2)}, u32[]{:S(2)}) %all-to-all-start) | async-done | bytes 1048608 | tf_op jit(solution)/shard_map/all_to_all | solution.py:373
  33.2 6.8 %shard_map.108 = (bf16[16,256,128]{2,1,0:T(8,128)(2,1)}, bf16[128,128]{1,0:T(8,128)(2,1)S(1)}, bf16[2,128,128]{2,1,0:T(8,128)(2,1)S(1)}, bf16[2,128,128]{2,1,0:T...) custom-call(bf16[16,256,128]{2,1,0:T(8,128)(2,1)S(1)} %all-to-all-do, ...), custom_call_target="tpu_custom_call" | custom-call | tf_op jit(solution)/shard_map/pallas_call | solution.py:46
  40.1 0.1 collective-permute-start.9
  40.2 4.6 %all-to-all-start.1 = ((bf16[16,256,128]{2,1,0:T(8,128)(2,1)}), bf16[16,256,128]{2,1,0:T(8,128)(2,1)S(1)}, u32[]{:S(2)}, u32[]{:S(2)}) async-start(bf16[16,256,128]{2,1,0:T(8,128)(2,1)} %get-tuple-element.23), calls=%async_computation.1 | async-start | bytes 2097152 | tf_op jit(solution)/shard_map/all_to_all | solution.py:382
  44.8 0.0 collective-permute-done.9.got
  44.8 0.1 shard_map.109
  44.8 4.5 %collective-permute-start.10 = (bf16[2,128,128]{2,1,0:T(8,128)(2,1)S(1)}, bf16[2,128,128]{2,1,0:T(8,128)(2,1)S(1)}, u32[]{:S(2)}, u32[]{:S(2)}) collective-permute-start(bf16[2,128,128]{2,1,0:T(8,128)(2,1)S(1)} %get-tuple-element.31), channel_id=1, source_target_pairs={{0,32},{1,33},{2,34},{3,35},{4,36},{5,37},{6,38},{7,39},{8,232},{9... | collective-permute-start | bytes 196616 | tf_op jit(solution)/shard_map/ppermute | solution.py:368
  49.3 2.0 %collective-permute-start.11 = (bf16[2,128,128]{2,1,0:T(8,128)(2,1)S(1)}, bf16[2,128,128]{2,1,0:T(8,128)(2,1)S(1)}, u32[]{:S(2)}, u32[]{:S(2)}) collective-permute-start(bf16[2,128,128]{2,1,0:T(8,128)(2,1)S(1)} %get-tuple-element.32), channel_id=1, source_target_pairs={{0,64},{1,65},{2,66},{3,67},{4,68},{5,69},{6,70},{7,71},{8,200},{9... | collective-permute-start | bytes 196616 | tf_op jit(solution)/shard_map/ppermute | solution.py:368
  51.4 3.7 %collective-permute-start.12 = (bf16[2,128,128]{2,1,0:T(8,128)(2,1)S(1)}, bf16[2,128,128]{2,1,0:T(8,128)(2,1)S(1)}, u32[]{:S(2)}, u32[]{:S(2)}) collective-permute-start(bf16[2,128,128]{2,1,0:T(8,128)(2,1)S(1)} %get-tuple-element.33), channel_id=1, source_target_pairs={{0,96},{1,97},{2,98},{3,99},{4,100},{5,101},{6,102},{7,103},{8,168... | collective-permute-start | bytes 196616 | tf_op jit(solution)/shard_map/ppermute | solution.py:368
  55.1 1.3 %collective-permute-start.13 = (bf16[128,128]{1,0:T(8,128)(2,1)S(1)}, bf16[128,128]{1,0:T(8,128)(2,1)S(1)}, u32[]{:S(2)}, u32[]{:S(2)}) collective-permute-start(bf16[128,128]{1,0:T(8,128)(2,1)S(1)} %get-tuple-element.34), channel_id=1, source_target_pairs={{0,128},{1,129},{2,130},{3,131},{4,132},{5,133},{6,134},{7,135},{8... | collective-permute-start | bytes 98312 | tf_op jit(solution)/shard_map/ppermute | solution.py:368
  56.4 1.6 %collective-permute-done.13.e4 = bf16[128,128]{1,0:T(8,128)(2,1)S(1)} collective-permute-done((bf16[128,128]{1,0:T(8,128)(2,1)S(1)}, bf16[128,128]{1,0:T(8,128)(2,1)S(1)}, u32[]{:S(2)}, u32[]{:S(2)}) %collective-permute-start.13) | collective-permute-done | bytes 32800 | tf_op jit(solution)/shard_map/ppermute | solution.py:368
  58.0 0.0 collective-permute-done.10.e1
  58.0 0.0 collective-permute-done.11.e2
  58.0 0.0 collective-permute-done.12.e3
  58.0 0.1 collective-permute-start.14
  58.1 1.2 %collective-permute-done.14.got = bf16[128,128]{1,0:T(8,128)(2,1)S(1)} collective-permute-done((bf16[128,128]{1,0:T(8,128)(2,1)S(1)}, bf16[128,128]{1,0:T(8,128)(2,1)S(1)}, u32[]{:S(2)}, u32[]{:S(2)}) %collective-permute-start.14) | collective-permute-done | bytes 32800 | tf_op jit(solution)/shard_map/ppermute | solution.py:365
  59.3 4.1 %all-to-all-done.1.dkv_all = bf16[16,256,128]{2,1,0:T(8,128)(2,1)S(1)} async-done(((bf16[16,256,128]{2,1,0:T(8,128)(2,1)}), bf16[16,256,128]{2,1,0:T(8,128)(2,1)S(1)}, u32[]{:S(2)}, u32[]{:S(2)}) %all-to-all-start.1) | async-done | bytes 1048608 | tf_op jit(solution)/shard_map/all_to_all | solution.py:382
  63.4 0.8 %shard_map.111 = (bf16[128,128]{1,0:T(8,128)(2,1)}, bf16[128,128]{1,0:T(8,128)(2,1)}, bf16[128,128]{1,0:T(8,128)(2,1)}) custom-call(bf16[16,256,128]{2,1,0:T(8,128)(2,1)S(1)} %all-to-all-done.1.dkv_all, f32[128,128]{1,0:T(8,128)S(1)} %get-tuple-element.35.keep, bf16[128,128]{1,0:T(8,128)(2,1)S(1)} %collective-permute-done.14.got), custom_call_target="tpu_custom_call" | custom-call | tf_op jit(solution)/shard_map/pallas_call | solution.py:46
  (1 shorter events, 0.0 us)
Async XLA Ops:
  2.2 2.1 %copy-start = (bf16[272,128]{1,0:T(8,128)(2,1)S(1)}, bf16[272,128]{1,0:T(8,128)(2,1)}, u32[]{:S(2)}) copy-start(bf16[272,128]{1,0:T(8,128)(2,1)} %shard_map.104.own_ref) | copy-start | bytes 208900
  2.2 2.0 %collective-permute-start = (bf16[272,128]{1,0:T(8,128)(2,1)}, bf16[272,128]{1,0:T(8,128)(2,1)S(1)}, u32[]{:S(2)}, u32[]{:S(2)}) collective-permute-start(bf16[272,128]{1,0:T(8,128)(2,1)} %shard_map.104.own_ref), channel_id=1, source_target_pairs={{0,8},{8,0},{1,9},{9,1},{2,10},{10,2},{3,11},{11,3},{4,12},{12,4},... | collective-permute-start | bytes 208904 | tf_op jit(solution)/shard_map/ppermute | solution.py:365
  4.5 23.7 %copy-start.1 = (s32[16,16]{1,0:T(8,128)S(1)}, s32[16,16]{1,0:T(8,128)}, u32[]{:S(2)}) copy-start(s32[16,16]{1,0:T(8,128)} %allow_hbm.1) | copy-start | bytes 3076
  4.5 23.7 %copy-start.2 = (s32[16]{0:T(128)S(1)}, s32[16]{0:T(128)}, u32[]{:S(2)}) copy-start(s32[16]{0:T(128)} %len_hbm.1) | copy-start | bytes 196
  4.5 13.8 %collective-permute-start.3 = (bf16[2,272,128]{2,1,0:T(8,128)(2,1)S(1)}, bf16[2,272,128]{2,1,0:T(8,128)(2,1)S(1)}, u32[]{:S(2)}, u32[]{:S(2)}) collective-permute-start(bf16[2,272,128]{2,1,0:T(8,128)(2,1)S(1)} %shard_map.105), channel_id=1, source_target_pairs={{96,0},{97,1},{98,2},{99,3},{100,4},{101,5},{102,6},{103,7},{168,8... | collective-permute-start | bytes 417800 | tf_op jit(solution)/shard_map/ppermute | solution.py:368
  5.8 13.3 %collective-permute-start.2 = (bf16[2,272,128]{2,1,0:T(8,128)(2,1)S(1)}, bf16[2,272,128]{2,1,0:T(8,128)(2,1)S(1)}, u32[]{:S(2)}, u32[]{:S(2)}) collective-permute-start(bf16[2,272,128]{2,1,0:T(8,128)(2,1)S(1)} %shard_map.105), channel_id=1, source_target_pairs={{64,0},{65,1},{66,2},{67,3},{68,4},{69,5},{70,6},{71,7},{200,8},{2... | collective-permute-start | bytes 417800 | tf_op jit(solution)/shard_map/ppermute | solution.py:368
  7.1 13.1 %collective-permute-start.1 = (bf16[2,272,128]{2,1,0:T(8,128)(2,1)S(1)}, bf16[2,272,128]{2,1,0:T(8,128)(2,1)S(1)}, u32[]{:S(2)}, u32[]{:S(2)}) collective-permute-start(bf16[2,272,128]{2,1,0:T(8,128)(2,1)S(1)} %shard_map.105), channel_id=1, source_target_pairs={{32,0},{33,1},{34,2},{35,3},{36,4},{37,5},{38,6},{39,7},{232,8},{2... | collective-permute-start | bytes 417800 | tf_op jit(solution)/shard_map/ppermute | solution.py:368
  10.9 22.4 %all-to-all-start = ((bf16[16,256,128]{2,1,0:T(8,128)(2,1)}), bf16[16,256,128]{2,1,0:T(8,128)(2,1)S(1)}, u32[]{:S(2)}, u32[]{:S(2)}) async-start(bf16[16,256,128]{2,1,0:T(8,128)(2,1)} %shard_map.103.after), calls=%async_computation | async-start | bytes 2097152 | tf_op jit(solution)/shard_map/all_to_all | solution.py:373
  16.2 12.0 %collective-permute-start.4 = (bf16[272,128]{1,0:T(8,128)(2,1)S(1)}, bf16[272,128]{1,0:T(8,128)(2,1)S(1)}, u32[]{:S(2)}, u32[]{:S(2)}) collective-permute-start(bf16[272,128]{1,0:T(8,128)(2,1)S(1)} %copy-done), channel_id=1, source_target_pairs={{128,0},{129,1},{130,2},{131,3},{132,4},{133,5},{134,6},{135,7},{1... | collective-permute-start | bytes 208904 | tf_op jit(solution)/shard_map/ppermute | solution.py:368
  18.3 11.2 %collective-permute-start.7 = (bf16[2,272,128]{2,1,0:T(8,128)(2,1)S(1)}, bf16[2,272,128]{2,1,0:T(8,128)(2,1)S(1)}, u32[]{:S(2)}, u32[]{:S(2)}) collective-permute-start(bf16[2,272,128]{2,1,0:T(8,128)(2,1)S(1)} %collective-permute-done.3.m3_ref), channel_id=1, source_target_pairs={{0,8},{8,0},{1,9},{9,1},{2,10},{10,2},{3,11},{11,3},{4,12},{12,4},... | collective-permute-start | bytes 417800 | tf_op jit(solution)/shard_map/ppermute | solution.py:365
  19.1 10.4 %collective-permute-start.6 = (bf16[2,272,128]{2,1,0:T(8,128)(2,1)S(1)}, bf16[2,272,128]{2,1,0:T(8,128)(2,1)S(1)}, u32[]{:S(2)}, u32[]{:S(2)}) collective-permute-start(bf16[2,272,128]{2,1,0:T(8,128)(2,1)S(1)} %collective-permute-done.2.m2_ref), channel_id=1, source_target_pairs={{0,8},{8,0},{1,9},{9,1},{2,10},{10,2},{3,11},{11,3},{4,12},{12,4},... | collective-permute-start | bytes 417800 | tf_op jit(solution)/shard_map/ppermute | solution.py:365
  20.2 9.2 %collective-permute-start.5 = (bf16[2,272,128]{2,1,0:T(8,128)(2,1)S(1)}, bf16[2,272,128]{2,1,0:T(8,128)(2,1)S(1)}, u32[]{:S(2)}, u32[]{:S(2)}) collective-permute-start(bf16[2,272,128]{2,1,0:T(8,128)(2,1)S(1)} %collective-permute-done.1.m1_ref.after), channel_id=1, source_target_pairs={{0,8},{8,0},{1,9},{9,1},{2,10},{10,2},{3,11},{11,3},{4,12},{12,4},... | collective-permute-start | bytes 417800 | tf_op jit(solution)/shard_map/ppermute | solution.py:365
  28.2 1.3 %collective-permute-start.8 = (bf16[272,128]{1,0:T(8,128)(2,1)S(1)}, bf16[272,128]{1,0:T(8,128)(2,1)S(1)}, u32[]{:S(2)}, u32[]{:S(2)}) collective-permute-start(bf16[272,128]{1,0:T(8,128)(2,1)S(1)} %collective-permute-done.4.m4_ref), channel_id=1, source_target_pairs={{0,8},{8,0},{1,9},{9,1},{2,10},{10,2},{3,11},{11,3},{4,12},{12,4},... | collective-permute-start | bytes 208904 | tf_op jit(solution)/shard_map/ppermute | solution.py:365
  40.1 4.7 %collective-permute-start.9 = (bf16[8,128,128]{2,1,0:T(8,128)(2,1)S(1)}, bf16[8,128,128]{2,1,0:T(8,128)(2,1)S(1)}, u32[]{:S(2)}, u32[]{:S(2)}) collective-permute-start(bf16[8,128,128]{2,1,0:T(8,128)(2,1)S(1)} %get-tuple-element.29), channel_id=1, source_target_pairs={{0,8},{8,0},{1,9},{9,1},{2,10},{10,2},{3,11},{11,3},{4,12},{12,4},... | collective-permute-start | bytes 786440 | tf_op jit(solution)/shard_map/ppermute | solution.py:365
  40.2 23.2 %all-to-all-start.1 = ((bf16[16,256,128]{2,1,0:T(8,128)(2,1)}), bf16[16,256,128]{2,1,0:T(8,128)(2,1)S(1)}, u32[]{:S(2)}, u32[]{:S(2)}) async-start(bf16[16,256,128]{2,1,0:T(8,128)(2,1)} %get-tuple-element.23), calls=%async_computation.1 | async-start | bytes 2097152 | tf_op jit(solution)/shard_map/all_to_all | solution.py:382
  44.8 13.1 %collective-permute-start.10 = (bf16[2,128,128]{2,1,0:T(8,128)(2,1)S(1)}, bf16[2,128,128]{2,1,0:T(8,128)(2,1)S(1)}, u32[]{:S(2)}, u32[]{:S(2)}) collective-permute-start(bf16[2,128,128]{2,1,0:T(8,128)(2,1)S(1)} %get-tuple-element.31), channel_id=1, source_target_pairs={{0,32},{1,33},{2,34},{3,35},{4,36},{5,37},{6,38},{7,39},{8,232},{9... | collective-permute-start | bytes 196616 | tf_op jit(solution)/shard_map/ppermute | solution.py:368
  49.3 8.6 %collective-permute-start.11 = (bf16[2,128,128]{2,1,0:T(8,128)(2,1)S(1)}, bf16[2,128,128]{2,1,0:T(8,128)(2,1)S(1)}, u32[]{:S(2)}, u32[]{:S(2)}) collective-permute-start(bf16[2,128,128]{2,1,0:T(8,128)(2,1)S(1)} %get-tuple-element.32), channel_id=1, source_target_pairs={{0,64},{1,65},{2,66},{3,67},{4,68},{5,69},{6,70},{7,71},{8,200},{9... | collective-permute-start | bytes 196616 | tf_op jit(solution)/shard_map/ppermute | solution.py:368
  51.4 6.6 %collective-permute-start.12 = (bf16[2,128,128]{2,1,0:T(8,128)(2,1)S(1)}, bf16[2,128,128]{2,1,0:T(8,128)(2,1)S(1)}, u32[]{:S(2)}, u32[]{:S(2)}) collective-permute-start(bf16[2,128,128]{2,1,0:T(8,128)(2,1)S(1)} %get-tuple-element.33), channel_id=1, source_target_pairs={{0,96},{1,97},{2,98},{3,99},{4,100},{5,101},{6,102},{7,103},{8,168... | collective-permute-start | bytes 196616 | tf_op jit(solution)/shard_map/ppermute | solution.py:368
  55.1 2.9 %collective-permute-start.13 = (bf16[128,128]{1,0:T(8,128)(2,1)S(1)}, bf16[128,128]{1,0:T(8,128)(2,1)S(1)}, u32[]{:S(2)}, u32[]{:S(2)}) collective-permute-start(bf16[128,128]{1,0:T(8,128)(2,1)S(1)} %get-tuple-element.34), channel_id=1, source_target_pairs={{0,128},{1,129},{2,130},{3,131},{4,132},{5,133},{6,134},{7,135},{8... | collective-permute-start | bytes 98312 | tf_op jit(solution)/shard_map/ppermute | solution.py:368
  58.0 1.3 %collective-permute-start.14 = (bf16[128,128]{1,0:T(8,128)(2,1)S(1)}, bf16[128,128]{1,0:T(8,128)(2,1)S(1)}, u32[]{:S(2)}, u32[]{:S(2)}) collective-permute-start(bf16[128,128]{1,0:T(8,128)(2,1)S(1)} %get-tuple-element.36), channel_id=1, source_target_pairs={{0,8},{8,0},{1,9},{9,1},{2,10},{10,2},{3,11},{11,3},{4,12},{12,4},... | collective-permute-start | bytes 98312 | tf_op jit(solution)/shard_map/ppermute | solution.py:365

commit v3 on v2

--- a/solution.py
+++ b/solution.py
@@ -221,7 +221,7 @@
 
 
 def slots_kernel(
-    own_ref, own_x_ref, m1_ref, m2_ref, m3_ref, m4_ref, x1_ref, x2_ref, x3_ref, x4_ref,
+    own_ref, own_x_ref, m4_ref, m3_ref, m2_ref, m1_ref, x4_ref, x3_ref, x2_ref, x1_ref,
     q_ref, g_ref, st_ref,
 ):
     slots = (
@@ -375,9 +375,9 @@
     mine = [along_z(both, k, back=True) for k in (1, 2, 3)]
     mine.append(along_z(own, 4, both_ways=False, back=True))
     at = plan(doc_lengths, tile_allowed, mine[0])
-    theirs = [swap(m) for m in mine]
-
-    q, g, stats = slots(own, own_x, *mine, *theirs)
+    theirs = [swap(m) for m in mine[::-1]][::-1]
+
+    q, g, stats = slots(own, own_x, *mine[::-1], *theirs[::-1])
     dkv, d0, d1, d2, d3, d4, dx = grads(kv, q, g, stats, at)
     dkv_all = lax.all_to_all(dkv, PLANE, 0, 0, tiled=True)
     s0, s1, s2, s3, s4 = call(

time: 65.4 us -> 64.7 us (0.989)
  waiting for transfers between devices: 20.4 us -> 19.2 us
  starting transfers between devices: 30.4 us -> 31.5 us
    ppermute x8, waiting for transfers between devices: 11.1 us -> 9.06 us  [along_z(): return lax.ppermute(x, AXES, pairs_along_z(k, both_ways, back))]
    ppermute x7, starting transfers between devices: 1.42 us -> 2.87 us  [swap(): return lax.ppermute(x, 'c', [(0, 1), (1, 0)])]
    all_to_all x1, starting transfers between devices: 4.59 us -> 3.66 us  [on_device(): dkv_all = lax.all_to_all(dkv, PLANE, 0, 0, tiled=True)]
  transfers between devices with their start and end apart: 17 -> 17, of which waited for: 8 -> 7; matrix products, arithmetic and copies ran while one was open for 0% -> 0% of each run, Pallas kernels for 5% -> 5%
where the time goes in v3:
time: 64.7 us; the launch traced here: 64 us
  starting transfers between devices  31.5 us (49%)
  waiting for transfers between devices  19.2 us (30%)
  Pallas kernels  12.4 us (19%)
  between operations  0.87 us (1%)
    ppermute x8, starting transfers between devices, along_z(): return lax.ppermute(x, AXES, pairs_along_z(k, both_ways, back))  19.6 us
    ppermute x8, waiting for transfers between devices, along_z(): return lax.ppermute(x, AXES, pairs_along_z(k, both_ways, back))  9.06 us
    pallas_call x5, Pallas kernels, call(): pl.pallas_call(body, out_shape=out_shape, in_specs=specs, **{} if out_spe...  7.81 us
    all_to_all x1, starting transfers between devices, on_device(): kv = lax.all_to_all(kv_out, PLANE, 0, 0, tiled=True)  5.31 us
    all_to_all x1, waiting for transfers between devices, on_device(): dkv_all = lax.all_to_all(dkv, PLANE, 0, 0, tiled=True)  4.37 us
    all_to_all x1, waiting for transfers between devices, on_device(): kv = lax.all_to_all(kv_out, PLANE, 0, 0, tiled=True)  4.29 us
    all_to_all x1, starting transfers between devices, on_device(): dkv_all = lax.all_to_all(dkv, PLANE, 0, 0, tiled=True)  3.66 us
    ppermute x7, starting transfers between devices, swap(): return lax.ppermute(x, 'c', [(0, 1), (1, 0)])  2.87 us
  transfers between devices with their start and end apart: 17, of which 7 were waited for; matrix products, arithmetic and copies ran while one was open for 0% of the time, Pallas kernels for 5%

profile of v3, /device:TPU:32, one launch (start us, length us, event | category | flops | bytes accessed | tf_op | source)
XLA Modules:
  0.0 64.0 jit_solution(9265237308761590539)
XLA Ops:
  0.6 1.6 %shard_map.104.own_ref = bf16[272,128]{1,0:T(8,128)(2,1)} custom-call(bf16[128,128]{1,0:T(8,128)(2,1)} %q_hbm.1, bf16[128,128]{1,0:T(8,128)(2,1)} %g_hbm.1, bf16[128,128]{1,0:T(8,128)(2,1)} %o_hbm.1, f32[1,128]{1,0:T(1,128)} %bitcast.1), custom_call_target="tpu_custom_call" | custom-call | tf_op jit(solution)/shard_map/pallas_call | solution.py:98
  2.2 0.0 copy-start
  2.2 0.1 collective-permute-start
  2.3 1.9 %shard_map.103.after = bf16[16,256,128]{2,1,0:T(8,128)(2,1)} custom-call(bf16[128,128]{1,0:T(8,128)(2,1)} %k_hbm.1, bf16[128,128]{1,0:T(8,128)(2,1)} %v_hbm.1), custom_call_target="tpu_custom_call" | custom-call | flops 1000000000 | bytes 2097152 | tf_op jit(solution)/shard_map/pallas_call | solution.py:190
  4.2 0.0 collective-permute-done.other_ref.own_x_ref
  4.3 0.0 copy-done
  4.3 0.2 shard_map.105
  4.5 0.0 copy-start.1
  4.5 0.0 copy-start.2
  4.5 3.8 %collective-permute-start.4 = (bf16[2,272,128]{2,1,0:T(8,128)(2,1)S(1)}, bf16[2,272,128]{2,1,0:T(8,128)(2,1)S(1)}, u32[]{:S(2)}, u32[]{:S(2)}) collective-permute-start(bf16[2,272,128]{2,1,0:T(8,128)(2,1)S(1)} %shard_map.105), channel_id=1, source_target_pairs={{32,0},{33,1},{34,2},{35,3},{36,4},{37,5},{38,6},{39,7},{232,8},{2... | collective-permute-start | bytes 417800 | tf_op jit(solution)/shard_map/ppermute | solution.py:368
  8.3 1.3 %collective-permute-start.3 = (bf16[2,272,128]{2,1,0:T(8,128)(2,1)S(1)}, bf16[2,272,128]{2,1,0:T(8,128)(2,1)S(1)}, u32[]{:S(2)}, u32[]{:S(2)}) collective-permute-start(bf16[2,272,128]{2,1,0:T(8,128)(2,1)S(1)} %shard_map.105), channel_id=1, source_target_pairs={{64,0},{65,1},{66,2},{67,3},{68,4},{69,5},{70,6},{71,7},{200,8},{2... | collective-permute-start | bytes 417800 | tf_op jit(solution)/shard_map/ppermute | solution.py:368
  9.6 1.3 %collective-permute-start.2 = (bf16[2,272,128]{2,1,0:T(8,128)(2,1)S(1)}, bf16[2,272,128]{2,1,0:T(8,128)(2,1)S(1)}, u32[]{:S(2)}, u32[]{:S(2)}) collective-permute-start(bf16[2,272,128]{2,1,0:T(8,128)(2,1)S(1)} %shard_map.105), channel_id=1, source_target_pairs={{96,0},{97,1},{98,2},{99,3},{100,4},{101,5},{102,6},{103,7},{168,8... | collective-permute-start | bytes 417800 | tf_op jit(solution)/shard_map/ppermute | solution.py:368
  10.9 5.3 %all-to-all-start = ((bf16[16,256,128]{2,1,0:T(8,128)(2,1)}), bf16[16,256,128]{2,1,0:T(8,128)(2,1)S(1)}, u32[]{:S(2)}, u32[]{:S(2)}) async-start(bf16[16,256,128]{2,1,0:T(8,128)(2,1)} %shard_map.103.after), calls=%async_computation | async-start | bytes 2097152 | tf_op jit(solution)/shard_map/all_to_all | solution.py:373
  16.2 1.3 %collective-permute-start.1 = (bf16[272,128]{1,0:T(8,128)(2,1)S(1)}, bf16[272,128]{1,0:T(8,128)(2,1)S(1)}, u32[]{:S(2)}, u32[]{:S(2)}) collective-permute-start(bf16[272,128]{1,0:T(8,128)(2,1)S(1)} %copy-done), channel_id=1, source_target_pairs={{128,0},{129,1},{130,2},{131,3},{132,4},{133,5},{134,6},{135,7},{1... | collective-permute-start | bytes 208904 | tf_op jit(solution)/shard_map/ppermute | solution.py:368
  17.5 0.0 collective-permute-done.4.m1_ref.after
  17.5 0.1 collective-permute-start.8
  17.6 0.0 collective-permute-done.3.m2_ref
  17.6 2.5 %collective-permute-start.7 = (bf16[2,272,128]{2,1,0:T(8,128)(2,1)S(1)}, bf16[2,272,128]{2,1,0:T(8,128)(2,1)S(1)}, u32[]{:S(2)}, u32[]{:S(2)}) collective-permute-start(bf16[2,272,128]{2,1,0:T(8,128)(2,1)S(1)} %collective-permute-done.3.m2_ref), channel_id=1, source_target_pairs={{0,8},{8,0},{1,9},{9,1},{2,10},{10,2},{3,11},{11,3},{4,12},{12,4},... | collective-permute-start | bytes 417800 | tf_op jit(solution)/shard_map/ppermute | solution.py:365
  20.1 1.2 %collective-permute-done.2.m3_ref = bf16[2,272,128]{2,1,0:T(8,128)(2,1)S(1)} collective-permute-done((bf16[2,272,128]{2,1,0:T(8,128)(2,1)S(1)}, bf16[2,272,128]{2,1,0:T(8,128)(2,1)S(1)}, u32[]{:S(2)}, u32[]{:S(2)}) %collective-permute-start.2) | collective-permute-done | bytes 139296 | tf_op jit(solution)/shard_map/ppermute | solution.py:368
  21.3 0.0 collective-permute-start.6
  21.4 6.2 %collective-permute-done.1.m4_ref = bf16[272,128]{1,0:T(8,128)(2,1)S(1)} collective-permute-done((bf16[272,128]{1,0:T(8,128)(2,1)S(1)}, bf16[272,128]{1,0:T(8,128)(2,1)S(1)}, u32[]{:S(2)}, u32[]{:S(2)}) %collective-permute-start.1) | collective-permute-done | bytes 69664 | tf_op jit(solution)/shard_map/ppermute | solution.py:368
  27.6 0.0 collective-permute-start.5
  27.6 0.0 copy-done.1
  27.6 0.0 copy-done.2
  27.6 0.9 %shard_map.107.at_ref = s32[9,8,256]{2,1,0:T(8,128)S(1)} custom-call(s32[16]{0:T(128)S(1)} %copy-done.2, s32[16,16]{1,0:T(8,128)S(1)} %copy-done.1, bf16[2,272,128]{2,1,0:T(8,128)(2,1)S(1)} %collective-permute-done.4.m1_ref.after), custom_call_target="tpu_custom_call" | custom-call | flops 1000000000 | bytes 2097152 | tf_op jit(solution)/shard_map/pallas_call | solution.py:157
  28.5 0.3 collective-permute-done.5.x4_ref
  28.8 0.0 collective-permute-done.8.x1_ref
  28.8 0.0 collective-permute-done.7.x2_ref
  28.8 0.0 collective-permute-done.6.x3_ref
  28.8 0.1 shard_map.106
  28.9 4.3 %all-to-all-done.kv_ref = bf16[16,256,128]{2,1,0:T(8,128)(2,1)S(1)} async-done(((bf16[16,256,128]{2,1,0:T(8,128)(2,1)}), bf16[16,256,128]{2,1,0:T(8,128)(2,1)S(1)}, u32[]{:S(2)}, u32[]{:S(2)}) %all-to-all-start) | async-done | bytes 1048608 | tf_op jit(solution)/shard_map/all_to_all | solution.py:373
  33.2 6.8 %shard_map.108 = (bf16[16,256,128]{2,1,0:T(8,128)(2,1)}, bf16[128,128]{1,0:T(8,128)(2,1)S(1)}, bf16[2,128,128]{2,1,0:T(8,128)(2,1)S(1)}, bf16[2,128,128]{2,1,0:T...) custom-call(bf16[16,256,128]{2,1,0:T(8,128)(2,1)S(1)} %all-to-all-do, ...), custom_call_target="tpu_custom_call" | custom-call | tf_op jit(solution)/shard_map/pallas_call | solution.py:46
  40.1 0.1 collective-permute-start.9
  40.2 3.7 %all-to-all-start.1 = ((bf16[16,256,128]{2,1,0:T(8,128)(2,1)}), bf16[16,256,128]{2,1,0:T(8,128)(2,1)S(1)}, u32[]{:S(2)}, u32[]{:S(2)}) async-start(bf16[16,256,128]{2,1,0:T(8,128)(2,1)} %get-tuple-element.23), calls=%async_computation.1 | async-start | bytes 2097152 | tf_op jit(solution)/shard_map/all_to_all | solution.py:382
  43.8 0.0 collective-permute-done.9.got
  43.9 0.1 shard_map.109
  43.9 2.9 %collective-permute-start.10 = (bf16[2,128,128]{2,1,0:T(8,128)(2,1)S(1)}, bf16[2,128,128]{2,1,0:T(8,128)(2,1)S(1)}, u32[]{:S(2)}, u32[]{:S(2)}) collective-permute-start(bf16[2,128,128]{2,1,0:T(8,128)(2,1)S(1)} %get-tuple-element.31), channel_id=1, source_target_pairs={{0,32},{1,33},{2,34},{3,35},{4,36},{5,37},{6,38},{7,39},{8,232},{9... | collective-permute-start | bytes 196616 | tf_op jit(solution)/shard_map/ppermute | solution.py:368
  46.9 4.5 %collective-permute-start.11 = (bf16[2,128,128]{2,1,0:T(8,128)(2,1)S(1)}, bf16[2,128,128]{2,1,0:T(8,128)(2,1)S(1)}, u32[]{:S(2)}, u32[]{:S(2)}) collective-permute-start(bf16[2,128,128]{2,1,0:T(8,128)(2,1)S(1)} %get-tuple-element.32), channel_id=1, source_target_pairs={{0,64},{1,65},{2,66},{3,67},{4,68},{5,69},{6,70},{7,71},{8,200},{9... | collective-permute-start | bytes 196616 | tf_op jit(solution)/shard_map/ppermute | solution.py:368
  51.4 3.3 %collective-permute-start.12 = (bf16[2,128,128]{2,1,0:T(8,128)(2,1)S(1)}, bf16[2,128,128]{2,1,0:T(8,128)(2,1)S(1)}, u32[]{:S(2)}, u32[]{:S(2)}) collective-permute-start(bf16[2,128,128]{2,1,0:T(8,128)(2,1)S(1)} %get-tuple-element.33), channel_id=1, source_target_pairs={{0,96},{1,97},{2,98},{3,99},{4,100},{5,101},{6,102},{7,103},{8,168... | collective-permute-start | bytes 196616 | tf_op jit(solution)/shard_map/ppermute | solution.py:368
  54.7 1.3 %collective-permute-start.13 = (bf16[128,128]{1,0:T(8,128)(2,1)S(1)}, bf16[128,128]{1,0:T(8,128)(2,1)S(1)}, u32[]{:S(2)}, u32[]{:S(2)}) collective-permute-start(bf16[128,128]{1,0:T(8,128)(2,1)S(1)} %get-tuple-element.34), channel_id=1, source_target_pairs={{0,128},{1,129},{2,130},{3,131},{4,132},{5,133},{6,134},{7,135},{8... | collective-permute-start | bytes 98312 | tf_op jit(solution)/shard_map/ppermute | solution.py:368
  56.0 1.6 %collective-permute-done.13.e4 = bf16[128,128]{1,0:T(8,128)(2,1)S(1)} collective-permute-done((bf16[128,128]{1,0:T(8,128)(2,1)S(1)}, bf16[128,128]{1,0:T(8,128)(2,1)S(1)}, u32[]{:S(2)}, u32[]{:S(2)}) %collective-permute-start.13) | collective-permute-done | bytes 32800 | tf_op jit(solution)/shard_map/ppermute | solution.py:368
  57.5 0.0 collective-permute-done.10.e1
  57.5 0.0 collective-permute-done.11.e2
  57.5 0.0 collective-permute-done.12.e3
  57.6 0.1 collective-permute-start.14
  57.7 1.2 %collective-permute-done.14.got = bf16[128,128]{1,0:T(8,128)(2,1)S(1)} collective-permute-done((bf16[128,128]{1,0:T(8,128)(2,1)S(1)}, bf16[128,128]{1,0:T(8,128)(2,1)S(1)}, u32[]{:S(2)}, u32[]{:S(2)}) %collective-permute-start.14) | collective-permute-done | bytes 32800 | tf_op jit(solution)/shard_map/ppermute | solution.py:365
  58.9 4.4 %all-to-all-done.1.dkv_all = bf16[16,256,128]{2,1,0:T(8,128)(2,1)S(1)} async-done(((bf16[16,256,128]{2,1,0:T(8,128)(2,1)}), bf16[16,256,128]{2,1,0:T(8,128)(2,1)S(1)}, u32[]{:S(2)}, u32[]{:S(2)}) %all-to-all-start.1) | async-done | bytes 1048608 | tf_op jit(solution)/shard_map/all_to_all | solution.py:382
  63.3 0.8 %shard_map.111 = (bf16[128,128]{1,0:T(8,128)(2,1)}, bf16[128,128]{1,0:T(8,128)(2,1)}, bf16[128,128]{1,0:T(8,128)(2,1)}) custom-call(bf16[16,256,128]{2,1,0:T(8,128)(2,1)S(1)} %all-to-all-done.1.dkv_all, f32[128,128]{1,0:T(8,128)S(1)} %get-tuple-element.35.keep, bf16[128,128]{1,0:T(8,128)(2,1)S(1)} %collective-permute-done.14.got), custom_call_target="tpu_custom_call" | custom-call | tf_op jit(solution)/shard_map/pallas_call | solution.py:46
  (1 shorter events, 0.0 us)
Async XLA Ops:
  2.2 2.1 %copy-start = (bf16[272,128]{1,0:T(8,128)(2,1)S(1)}, bf16[272,128]{1,0:T(8,128)(2,1)}, u32[]{:S(2)}) copy-start(bf16[272,128]{1,0:T(8,128)(2,1)} %shard_map.104.own_ref) | copy-start | bytes 208900
  2.2 2.0 %collective-permute-start = (bf16[272,128]{1,0:T(8,128)(2,1)}, bf16[272,128]{1,0:T(8,128)(2,1)S(1)}, u32[]{:S(2)}, u32[]{:S(2)}) collective-permute-start(bf16[272,128]{1,0:T(8,128)(2,1)} %shard_map.104.own_ref), channel_id=1, source_target_pairs={{0,8},{8,0},{1,9},{9,1},{2,10},{10,2},{3,11},{11,3},{4,12},{12,4},... | collective-permute-start | bytes 208904 | tf_op jit(solution)/shard_map/ppermute | solution.py:365
  4.5 23.1 %copy-start.1 = (s32[16,16]{1,0:T(8,128)S(1)}, s32[16,16]{1,0:T(8,128)}, u32[]{:S(2)}) copy-start(s32[16,16]{1,0:T(8,128)} %allow_hbm.1) | copy-start | bytes 3076
  4.5 23.1 %copy-start.2 = (s32[16]{0:T(128)S(1)}, s32[16]{0:T(128)}, u32[]{:S(2)}) copy-start(s32[16]{0:T(128)} %len_hbm.1) | copy-start | bytes 196
  4.5 13.0 %collective-permute-start.4 = (bf16[2,272,128]{2,1,0:T(8,128)(2,1)S(1)}, bf16[2,272,128]{2,1,0:T(8,128)(2,1)S(1)}, u32[]{:S(2)}, u32[]{:S(2)}) collective-permute-start(bf16[2,272,128]{2,1,0:T(8,128)(2,1)S(1)} %shard_map.105), channel_id=1, source_target_pairs={{32,0},{33,1},{34,2},{35,3},{36,4},{37,5},{38,6},{39,7},{232,8},{2... | collective-permute-start | bytes 417800 | tf_op jit(solution)/shard_map/ppermute | solution.py:368
  8.3 9.3 %collective-permute-start.3 = (bf16[2,272,128]{2,1,0:T(8,128)(2,1)S(1)}, bf16[2,272,128]{2,1,0:T(8,128)(2,1)S(1)}, u32[]{:S(2)}, u32[]{:S(2)}) collective-permute-start(bf16[2,272,128]{2,1,0:T(8,128)(2,1)S(1)} %shard_map.105), channel_id=1, source_target_pairs={{64,0},{65,1},{66,2},{67,3},{68,4},{69,5},{70,6},{71,7},{200,8},{2... | collective-permute-start | bytes 417800 | tf_op jit(solution)/shard_map/ppermute | solution.py:368
  9.6 11.8 %collective-permute-start.2 = (bf16[2,272,128]{2,1,0:T(8,128)(2,1)S(1)}, bf16[2,272,128]{2,1,0:T(8,128)(2,1)S(1)}, u32[]{:S(2)}, u32[]{:S(2)}) collective-permute-start(bf16[2,272,128]{2,1,0:T(8,128)(2,1)S(1)} %shard_map.105), channel_id=1, source_target_pairs={{96,0},{97,1},{98,2},{99,3},{100,4},{101,5},{102,6},{103,7},{168,8... | collective-permute-start | bytes 417800 | tf_op jit(solution)/shard_map/ppermute | solution.py:368
  10.9 22.4 %all-to-all-start = ((bf16[16,256,128]{2,1,0:T(8,128)(2,1)}), bf16[16,256,128]{2,1,0:T(8,128)(2,1)S(1)}, u32[]{:S(2)}, u32[]{:S(2)}) async-start(bf16[16,256,128]{2,1,0:T(8,128)(2,1)} %shard_map.103.after), calls=%async_computation | async-start | bytes 2097152 | tf_op jit(solution)/shard_map/all_to_all | solution.py:373
  16.2 11.4 %collective-permute-start.1 = (bf16[272,128]{1,0:T(8,128)(2,1)S(1)}, bf16[272,128]{1,0:T(8,128)(2,1)S(1)}, u32[]{:S(2)}, u32[]{:S(2)}) collective-permute-start(bf16[272,128]{1,0:T(8,128)(2,1)S(1)} %copy-done), channel_id=1, source_target_pairs={{128,0},{129,1},{130,2},{131,3},{132,4},{133,5},{134,6},{135,7},{1... | collective-permute-start | bytes 208904 | tf_op jit(solution)/shard_map/ppermute | solution.py:368
  17.5 11.3 %collective-permute-start.8 = (bf16[2,272,128]{2,1,0:T(8,128)(2,1)S(1)}, bf16[2,272,128]{2,1,0:T(8,128)(2,1)S(1)}, u32[]{:S(2)}, u32[]{:S(2)}) collective-permute-start(bf16[2,272,128]{2,1,0:T(8,128)(2,1)S(1)} %collective-permute-done.4.m1_ref.after), channel_id=1, source_target_pairs={{0,8},{8,0},{1,9},{9,1},{2,10},{10,2},{3,11},{11,3},{4,12},{12,4},... | collective-permute-start | bytes 417800 | tf_op jit(solution)/shard_map/ppermute | solution.py:365
  17.6 11.2 %collective-permute-start.7 = (bf16[2,272,128]{2,1,0:T(8,128)(2,1)S(1)}, bf16[2,272,128]{2,1,0:T(8,128)(2,1)S(1)}, u32[]{:S(2)}, u32[]{:S(2)}) collective-permute-start(bf16[2,272,128]{2,1,0:T(8,128)(2,1)S(1)} %collective-permute-done.3.m2_ref), channel_id=1, source_target_pairs={{0,8},{8,0},{1,9},{9,1},{2,10},{10,2},{3,11},{11,3},{4,12},{12,4},... | collective-permute-start | bytes 417800 | tf_op jit(solution)/shard_map/ppermute | solution.py:365
  21.3 7.5 %collective-permute-start.6 = (bf16[2,272,128]{2,1,0:T(8,128)(2,1)S(1)}, bf16[2,272,128]{2,1,0:T(8,128)(2,1)S(1)}, u32[]{:S(2)}, u32[]{:S(2)}) collective-permute-start(bf16[2,272,128]{2,1,0:T(8,128)(2,1)S(1)} %collective-permute-done.2.m3_ref), channel_id=1, source_target_pairs={{0,8},{8,0},{1,9},{9,1},{2,10},{10,2},{3,11},{11,3},{4,12},{12,4},... | collective-permute-start | bytes 417800 | tf_op jit(solution)/shard_map/ppermute | solution.py:365
  27.6 1.3 %collective-permute-start.5 = (bf16[272,128]{1,0:T(8,128)(2,1)S(1)}, bf16[272,128]{1,0:T(8,128)(2,1)S(1)}, u32[]{:S(2)}, u32[]{:S(2)}) collective-permute-start(bf16[272,128]{1,0:T(8,128)(2,1)S(1)} %collective-permute-done.1.m4_ref), channel_id=1, source_target_pairs={{0,8},{8,0},{1,9},{9,1},{2,10},{10,2},{3,11},{11,3},{4,12},{12,4},... | collective-permute-start | bytes 208904 | tf_op jit(solution)/shard_map/ppermute | solution.py:365
  40.1 3.8 %collective-permute-start.9 = (bf16[8,128,128]{2,1,0:T(8,128)(2,1)S(1)}, bf16[8,128,128]{2,1,0:T(8,128)(2,1)S(1)}, u32[]{:S(2)}, u32[]{:S(2)}) collective-permute-start(bf16[8,128,128]{2,1,0:T(8,128)(2,1)S(1)} %get-tuple-element.29), channel_id=1, source_target_pairs={{0,8},{8,0},{1,9},{9,1},{2,10},{10,2},{3,11},{11,3},{4,12},{12,4},... | collective-permute-start | bytes 786440 | tf_op jit(solution)/shard_map/ppermute | solution.py:365
  40.2 23.1 %all-to-all-start.1 = ((bf16[16,256,128]{2,1,0:T(8,128)(2,1)}), bf16[16,256,128]{2,1,0:T(8,128)(2,1)S(1)}, u32[]{:S(2)}, u32[]{:S(2)}) async-start(bf16[16,256,128]{2,1,0:T(8,128)(2,1)} %get-tuple-element.23), calls=%async_computation.1 | async-start | bytes 2097152 | tf_op jit(solution)/shard_map/all_to_all | solution.py:382
  43.9 13.6 %collective-permute-start.10 = (bf16[2,128,128]{2,1,0:T(8,128)(2,1)S(1)}, bf16[2,128,128]{2,1,0:T(8,128)(2,1)S(1)}, u32[]{:S(2)}, u32[]{:S(2)}) collective-permute-start(bf16[2,128,128]{2,1,0:T(8,128)(2,1)S(1)} %get-tuple-element.31), channel_id=1, source_target_pairs={{0,32},{1,33},{2,34},{3,35},{4,36},{5,37},{6,38},{7,39},{8,232},{9... | collective-permute-start | bytes 196616 | tf_op jit(solution)/shard_map/ppermute | solution.py:368
  46.9 10.7 %collective-permute-start.11 = (bf16[2,128,128]{2,1,0:T(8,128)(2,1)S(1)}, bf16[2,128,128]{2,1,0:T(8,128)(2,1)S(1)}, u32[]{:S(2)}, u32[]{:S(2)}) collective-permute-start(bf16[2,128,128]{2,1,0:T(8,128)(2,1)S(1)} %get-tuple-element.32), channel_id=1, source_target_pairs={{0,64},{1,65},{2,66},{3,67},{4,68},{5,69},{6,70},{7,71},{8,200},{9... | collective-permute-start | bytes 196616 | tf_op jit(solution)/shard_map/ppermute | solution.py:368
  51.4 6.2 %collective-permute-start.12 = (bf16[2,128,128]{2,1,0:T(8,128)(2,1)S(1)}, bf16[2,128,128]{2,1,0:T(8,128)(2,1)S(1)}, u32[]{:S(2)}, u32[]{:S(2)}) collective-permute-start(bf16[2,128,128]{2,1,0:T(8,128)(2,1)S(1)} %get-tuple-element.33), channel_id=1, source_target_pairs={{0,96},{1,97},{2,98},{3,99},{4,100},{5,101},{6,102},{7,103},{8,168... | collective-permute-start | bytes 196616 | tf_op jit(solution)/shard_map/ppermute | solution.py:368
  54.7 2.9 %collective-permute-start.13 = (bf16[128,128]{1,0:T(8,128)(2,1)S(1)}, bf16[128,128]{1,0:T(8,128)(2,1)S(1)}, u32[]{:S(2)}, u32[]{:S(2)}) collective-permute-start(bf16[128,128]{1,0:T(8,128)(2,1)S(1)} %get-tuple-element.34), channel_id=1, source_target_pairs={{0,128},{1,129},{2,130},{3,131},{4,132},{5,133},{6,134},{7,135},{8... | collective-permute-start | bytes 98312 | tf_op jit(solution)/shard_map/ppermute | solution.py:368
  57.6 1.3 %collective-permute-start.14 = (bf16[128,128]{1,0:T(8,128)(2,1)S(1)}, bf16[128,128]{1,0:T(8,128)(2,1)S(1)}, u32[]{:S(2)}, u32[]{:S(2)}) collective-permute-start(bf16[128,128]{1,0:T(8,128)(2,1)S(1)} %get-tuple-element.36), channel_id=1, source_target_pairs={{0,8},{8,0},{1,9},{9,1},{2,10},{10,2},{3,11},{11,3},{4,12},{12,4},... | collective-permute-start | bytes 98312 | tf_op jit(solution)/shard_map/ppermute | solution.py:365
